TPU v7x, 512 devices: a whole 4x8x8 slice. The times are simulated.
512 devices in a mesh: rep: 64 (over y, z), tp: 8 (over x, core).
Axes of the slice: x: 4, y: 8, z: 8, core: 2. Of those that a mesh axis runs over, the one named last changes fastest.
Arguments:
- queries: bfloat16 [2048, 4, 8192], P('rep', None, 'tp'), may hold values from -400 to 400
- new_keys: bfloat16 [2048, 4, 1024], P('rep', None, 'tp'), may hold values from -8 to 8
- new_values: bfloat16 [2048, 4, 1024], P('rep', None, 'tp'), may hold values from -6 to 6
- key_pool: bfloat16 [8192, 64, 1024], P('rep', None, 'tp'), may hold values from -6 to 6
- value_pool: bfloat16 [8192, 64, 1024], P('rep', None, 'tp'), may hold values from -400 to 400
- block_table: int32 [2048, 2], P('rep'), may hold values from 0 to 127, as said below
- context: int32 [2048], P('rep'), may hold values from 1 to 128
- move_source: int32 [4096], P('rep'), may hold values from 0 to 127
- move_replica: int32 [4096], P('rep'), may hold values from 0 to 63, as said below
- move_target: int32 [4096], P('rep'), may hold values from 0 to 127, as said below
- norm_gain: float32 [8192], P('tp'), may hold values from 0.1 to 1.9
Outputs:
- normed: float32 [2048, 4, 8192], P('rep', None, 'tp')
Inputs may be any that keep to these rules, and one draw needn't show every extreme that they name: `block_table`: the 2 slots of the requests of one replica are distinct; no such slot is the move_source of an entry of that replica. An entry whose move_replica is its own replica has move_target equal to move_source. Any other entry moves its page to another replica; at most 2 such entries of one replica name the same receiving replica, and some replica sends exactly 2 to some other; one replica receives at most 64 pages, and some replica receives exactly 64. `move_target`: the targets of pages moved into one replica are distinct slots of that replica's block tables.
All inputs are finite; a program needn't handle non-finite values.
Results may differ from a plain program's by a relative error of at most 0.0022.
Values may be sent and summed in bfloat16 or wider, within the bound.
A program may use at most 64 MiB of HBM per device.

v0:
```python
import math

import jax
import jax.numpy as jnp
from jax import lax
from jax.sharding import PartitionSpec as P

QH = 64
KVH = 8
HD = 128
CAP = 2


MASKED = -1e30


def partials(grouped, key_blocks, value_blocks, allowed):
    scaling = 1.0 / math.sqrt(HD)
    scores = (
        jnp.einsum("rtkgd,rpjkd->rptkgj", grouped, key_blocks, preferred_element_type=jnp.float32)
        * scaling
    )
    scores = jnp.where(allowed[:, :, :, None, None, :], scores, MASKED)
    maxima = jnp.max(scores, axis=-1)
    weights = jnp.exp(scores - maxima[..., None])
    totals = jnp.sum(weights, axis=-1)
    accumulated = jnp.einsum(
        "rptkgj,rpjkd->rptkgd",
        weights.astype(jnp.bfloat16),
        value_blocks,
        preferred_element_type=jnp.float32,
    )
    return (maxima, totals, accumulated)


def combine(maxima, totals, accumulated):
    largest = jnp.max(maxima, axis=1)
    factors = jnp.exp(maxima - largest[:, None])
    numerator = jnp.sum(factors[..., None] * accumulated, axis=1)
    denominator = jnp.sum(factors * totals, axis=1)
    return numerator / denominator[..., None]


def bucket_ranks(replica_ids, moving):
    entry_count = replica_ids.shape[-1]
    matching = (replica_ids[..., :, None] == replica_ids[..., None, :]) & moving[..., None, :]
    earlier = jnp.arange(entry_count)[None, :] < jnp.arange(entry_count)[:, None]
    return jnp.sum(matching & earlier, axis=-1)


def per_device(
    queries,
    new_keys,
    new_values,
    key_pool,
    value_pool,
    block_table,
    context,
    move_source,
    move_replica,
    move_target,
    norm_gain,
):
    row_count, step_count, query_width = queries.shape
    page_count, page_length, key_width = key_pool.shape
    page_slots = block_table.shape[1]
    heads_here = key_width // HD
    group = QH // KVH
    replicas = lax.axis_size("rep")
    buckets = replicas * CAP
    replica_id = lax.axis_index("rep")
    moving = move_replica != replica_id
    bucket = jnp.where(moving, move_replica * CAP + bucket_ranks(move_replica, moving), buckets)
    selector = bucket[None, :] == jnp.arange(buckets, dtype=jnp.int32)[:, None]
    notice = jnp.where(
        jnp.any(selector, axis=1),
        jnp.sum(jnp.where(selector, move_target[None, :], 0), axis=1),
        page_count,
    )
    incoming = lax.all_to_all(
        notice.reshape(replicas, CAP), "rep", split_axis=0, concat_axis=0, tiled=True
    ).reshape(buckets)
    grouped = queries.reshape(row_count, step_count, heads_here, group, HD)
    positions = (
        jnp.arange(page_slots, dtype=jnp.int32)[:, None] * page_length
        + jnp.arange(page_length, dtype=jnp.int32)[None, :]
    )
    live_mask = positions[None] < context[:, None, None]
    cache_allowed = jnp.broadcast_to(
        live_mask[:, :, None, :], (row_count, page_slots, step_count, page_length)
    )
    shape_cache = (row_count, page_slots, page_length, heads_here, HD)
    entries = jnp.argmax(selector.astype(jnp.int32), axis=1)
    chosen_slot = move_source[entries]
    packed_keys = key_pool[chosen_slot].reshape(replicas, CAP, page_length, key_width)
    packed_values = value_pool[chosen_slot].reshape(replicas, CAP, page_length, key_width)
    got_keys, got_values = (
        lax.all_to_all(packed_keys, "rep", split_axis=0, concat_axis=0, tiled=True),
        lax.all_to_all(packed_values, "rep", split_axis=0, concat_axis=0, tiled=True),
    )
    keys_now = key_pool.at[incoming].set(
        got_keys.reshape(buckets, page_length, key_width), mode="drop"
    )
    values_now = value_pool.at[incoming].set(
        got_values.reshape(buckets, page_length, key_width), mode="drop"
    )
    maxima, totals, accumulated = partials(
        grouped,
        keys_now[block_table].reshape(shape_cache),
        values_now[block_table].reshape(shape_cache),
        cache_allowed,
    )
    causal = (
        jnp.arange(step_count, dtype=jnp.int32)[None, :]
        <= jnp.arange(step_count, dtype=jnp.int32)[:, None]
    )
    draft_allowed = jnp.broadcast_to(causal[None, None], (row_count, 1, step_count, step_count))
    shape_draft = (row_count, 1, step_count, heads_here, HD)
    draft_max, draft_total, draft_sum = partials(
        grouped, new_keys.reshape(shape_draft), new_values.reshape(shape_draft), draft_allowed
    )
    attention = combine(
        jnp.concatenate([maxima, draft_max], axis=1),
        jnp.concatenate([totals, draft_total], axis=1),
        jnp.concatenate([accumulated, draft_sum], axis=1),
    ).reshape(row_count, step_count, query_width)
    squares = lax.psum(jnp.sum(attention * attention, axis=-1), "tp")
    return attention * lax.rsqrt(squares / (QH * HD) + 1e-05)[..., None] * norm_gain


def solution(mesh):
    in_specs = (
        P("rep", None, "tp"),
        P("rep", None, "tp"),
        P("rep", None, "tp"),
        P("rep", None, "tp"),
        P("rep", None, "tp"),
        P("rep", None),
        P("rep"),
        P("rep"),
        P("rep"),
        P("rep"),
        P("tp"),
    )
    out_specs = P("rep", None, "tp")
    return jax.shard_map(
        per_device, mesh=mesh, in_specs=in_specs, out_specs=out_specs, check_vma=False
    )
```

profile of v0, /device:TPU:104, one launch (start us, length us, event | category | flops | bytes accessed | tf_op | source)
XLA Modules:
  0.0 189.5 jit_solution(13928021055571515355)
XLA Ops:
  0.0 3.2 %copy.83 = bf16[128,64,128]{2,1,0:T(8,128)(2,1)} copy(bf16[128,64,128]{2,1,0:T(8,128)(2,1)} %param.14) | data formatting | bytes 4194304
  4.3 0.8 select_n.70
  5.1 15.4 %all-to-all-start = ((s32[64,1,2]{2,1,0:T(1,128)}), s32[64,1,2]{2,1,0:T(1,128)S(1)}, u32[]{:S(2)}, u32[]{:S(2)}) async-start(s32[64,1,2]{2,1,0:T(1,128)} %bitcast), calls=%async_computation | async-start | bytes 65536 | tf_op jit(solution)/shard_map/all_to_all | solution.py:80
  20.5 0.7 iota_reduce_fusion
  21.2 1.2 gather_fusion
  22.4 3.7 %gather_fusion.1 = bf16[128,64,128]{2,1,0:T(8,128)(2,1)} fusion(bf16[128,64,128]{2,1,0:T(8,128)(2,1)} %copy.83, s32[1024]{0:T(1024)S(1)} %pad_clamp_fusion.1), kind=kCustom, calls=%fused_computation.1 | custom fusion | bytes 4194816 | tf_op jit(solution)/shard_map/gather | solution.py:95
  26.1 1.2 all-to-all-done
  27.4 11.7 %all-to-all-start.1 = ((bf16[64,2,64,128]{3,2,1,0:T(8,128)(2,1)}), bf16[64,2,64,128]{3,2,1,0:T(8,128)(2,1)}, u32[]{:S(2)}, u32[]{:S(2)}) async-start(bf16[64,2,64,128]{3,2,1,0:T(8,128)(2,1)} %bitcast.79), calls=%async_computation.1 | async-start | bytes 4194304 | tf_op jit(solution)/shard_map/all_to_all | solution.py:98
  39.0 2.2 %gather_fusion.3 = bf16[128,64,128]{2,1,0:T(8,128)(2,1)} fusion(bf16[128,64,128]{2,1,0:T(8,128)(2,1)S(1)} %copy.84, s32[1024]{0:T(1024)S(1)} %pad_clamp_fusion.1), kind=kCustom, calls=%fused_computation.3 | custom fusion | bytes 4194816 | tf_op jit(solution)/shard_map/gather | solution.py:96
  41.2 53.6 %all-to-all-done.1 = bf16[64,2,64,128]{3,2,1,0:T(8,128)(2,1)} async-done(((bf16[64,2,64,128]{3,2,1,0:T(8,128)(2,1)}), bf16[64,2,64,128]{3,2,1,0:T(8,128)(2,1)}, u32[]{:S(2)}, u32[]{:S(2)}) %all-to-all-start.1) | async-done | bytes 2097184 | tf_op jit(solution)/shard_map/all_to_all | solution.py:98
  94.8 8.2 %all-to-all-start.2 = ((bf16[64,2,64,128]{3,2,1,0:T(8,128)(2,1)}), bf16[64,2,64,128]{3,2,1,0:T(8,128)(2,1)}, u32[]{:S(2)}, u32[]{:S(2)}) async-start(bf16[64,2,64,128]{3,2,1,0:T(8,128)(2,1)} %bitcast.78), calls=%async_computation.2 | async-start | bytes 4194304 | tf_op jit(solution)/shard_map/all_to_all | solution.py:99
  103.1 0.8 reshape.402
  104.3 1.3 fusion.27
  106.5 0.7 copy.70
  108.5 1.1 convolution_bitcast_fusion.1
  110.4 0.7 reduce.36
  111.2 17.5 %scatter_fusion = bf16[128,64,128]{2,1,0:T(8,128)(2,1)} fusion(bf16[128,64,128]{2,1,0:T(8,128)(2,1)} %copy.83, s32[128]{0:T(128)S(1)} %fusion.25, bf16[128,64,128]{2,1,0:T(8,128)(2,1)} %bitcast.5), kind=kCustom, calls=%fused_computation.5 | custom fusion | bytes 6291968 | tf_op jit(solution)/shard_map/scatter | solution.py:101
  128.7 3.3 %gather_fusion.2 = bf16[64,64,128]{2,1,0:T(8,128)(2,1)} fusion(bf16[128,64,128]{2,1,0:T(8,128)(2,1)} %scatter_fusion, s32[1024]{0:T(1024)S(1)} %pad_clamp_fusion), kind=kCustom, calls=%fused_computation.2 | custom fusion | bytes 2097408 | tf_op jit(solution)/shard_map/gather | solution.py:109
  132.0 2.4 %fusion.28 = (f32[32,2,4,8]{3,2,1,0:T(4,128)S(1)}, f32[32,2,4,1,8,64]{5,4,2,1,0,3:T(8,128)S(1)}) fusion(bf16[32,2,64,128,1]{3,2,4,1,0:T(8,128)(2,1)} %bitcast.80, bf16[32,4,8,128,1]{3,2,1,0,4:T(8,128)(2,1)} %reshape.402, pred[32,2,64]{2,1,0:T(4,128)(4,1)S(1)} %broadcast_compare_fusion), kind=kOutput, calls=%fused_computation.65 | convolution fusion | flops 33945600 | bytes 1847296 | tf_op jit(solution)/shard_map/rtkgd,rpjkd->rptkgj/dot_general | solution.py:20
  134.6 1.0 fusion.6
  135.5 0.7 copy.64
  136.4 0.8 reduce_max.36
  137.2 0.8 fusion.20
  137.9 0.7 copy.71
  138.6 1.3 fusion.17
  140.0 0.9 copy.66
  140.9 17.1 %all-to-all-done.2 = bf16[64,2,64,128]{3,2,1,0:T(8,128)(2,1)} async-done(((bf16[64,2,64,128]{3,2,1,0:T(8,128)(2,1)}), bf16[64,2,64,128]{3,2,1,0:T(8,128)(2,1)}, u32[]{:S(2)}, u32[]{:S(2)}) %all-to-all-start.2) | async-done | bytes 2097184 | tf_op jit(solution)/shard_map/all_to_all | solution.py:99
  158.0 12.0 %scatter_fusion.1 = bf16[128,64,128]{2,1,0:T(8,128)(2,1)S(1)} fusion(bf16[128,64,128]{2,1,0:T(8,128)(2,1)S(1)} %copy.84, s32[128]{0:T(128)S(1)} %fusion.25, bf16[128,64,128]{2,1,0:T(8,128)(2,1)} %bitcast.18), kind=kCustom, calls=%fused_computation.6 | custom fusion | bytes 6291968 | tf_op jit(solution)/shard_map/scatter | solution.py:104
  170.0 1.7 gather_fusion.4
  171.7 1.7 convolution_bitcast_fusion
  175.0 13.5 %psum.7 = f32[32,4]{0,1:T(4,128)S(1)} all-reduce(f32[32,4]{0,1:T(4,128)S(1)} %copy.72), channel_id=1, replica_groups=mesh['rep'=64,'tp'=8] {'tp'}, use_global_device_ids=true, to_apply=%region_14.15 | all-reduce | flops 128 | bytes 1024 | tf_op jit(solution)/shard_map/psum | solution.py:127
  188.5 1.0 multiply_multiply_fusion
  (60 shorter events, 6.4 us)
Async XLA Ops:
  0.0 108.5 %copy-start = (bf16[32,4,128]{2,1,0:T(4,128)(2,1)S(1)}, bf16[32,4,128]{2,1,0:T(4,128)(2,1)}, u32[]{:S(2)}) copy-start(bf16[32,4,128]{2,1,0:T(4,128)(2,1)} %param.13) | copy-start | bytes 98308
  0.0 3.2 %copy-start.2 = (bf16[128,64,128]{2,1,0:T(8,128)(2,1)S(1)}, bf16[128,64,128]{2,1,0:T(8,128)(2,1)}, u32[]{:S(2)}) copy-start(bf16[128,64,128]{2,1,0:T(8,128)(2,1)} %param.15) | copy-start | bytes 6291460
  3.2 0.7 copy-start.6
  3.3 0.9 copy-start.11
  3.3 17.9 %copy-start.1 = (s32[64]{0:T(128)S(1)}, s32[64]{0:T(128)}, u32[]{:S(2)}) copy-start(s32[64]{0:T(128)} %param.18) | copy-start | bytes 772
  5.1 22.3 %all-to-all-start = ((s32[64,1,2]{2,1,0:T(1,128)}), s32[64,1,2]{2,1,0:T(1,128)S(1)}, u32[]{:S(2)}, u32[]{:S(2)}) async-start(s32[64,1,2]{2,1,0:T(1,128)} %bitcast), calls=%async_computation | async-start | bytes 65536 | tf_op jit(solution)/shard_map/all_to_all | solution.py:80
  27.4 67.5 %all-to-all-start.1 = ((bf16[64,2,64,128]{3,2,1,0:T(8,128)(2,1)}), bf16[64,2,64,128]{3,2,1,0:T(8,128)(2,1)}, u32[]{:S(2)}, u32[]{:S(2)}) async-start(bf16[64,2,64,128]{3,2,1,0:T(8,128)(2,1)} %bitcast.79), calls=%async_computation.1 | async-start | bytes 4194304 | tf_op jit(solution)/shard_map/all_to_all | solution.py:98
  94.8 8.3 %copy-start.4 = (bf16[32,4,1024]{2,1,0:T(4,128)(2,1)S(1)}, bf16[32,4,1024]{2,1,0:T(4,128)(2,1)}, u32[]{:S(2)}) copy-start(bf16[32,4,1024]{2,1,0:T(4,128)(2,1)} %param.11) | copy-start | bytes 786436
  94.8 9.2 %copy-start.8 = (s32[32,2]{0,1:T(2,128)S(1)}, s32[32,2]{0,1:T(2,128)}, u32[]{:S(2)}) copy-start(s32[32,2]{0,1:T(2,128)} %param.16) | copy-start | bytes 772
  94.8 9.4 %copy-start.10 = (bf16[32,4,128]{2,1,0:T(4,128)(2,1)S(1)}, bf16[32,4,128]{2,1,0:T(4,128)(2,1)}, u32[]{:S(2)}) copy-start(bf16[32,4,128]{2,1,0:T(4,128)(2,1)} %param.12) | copy-start | bytes 98308
  94.8 63.2 %all-to-all-start.2 = ((bf16[64,2,64,128]{3,2,1,0:T(8,128)(2,1)}), bf16[64,2,64,128]{3,2,1,0:T(8,128)(2,1)}, u32[]{:S(2)}, u32[]{:S(2)}) async-start(bf16[64,2,64,128]{3,2,1,0:T(8,128)(2,1)} %bitcast.78), calls=%async_computation.2 | async-start | bytes 4194304 | tf_op jit(solution)/shard_map/all_to_all | solution.py:99
  103.1 6.6 %copy-start.9 = (s32[32]{0:T(128)S(1)}, s32[32]{0:T(128)}, u32[]{:S(2)}) copy-start(s32[32]{0:T(128)} %param.17) | copy-start | bytes 388
  171.7 1.7 copy-start.3
  173.4 0.8 copy-start.5
  173.4 15.1 %copy-start.7 = (f32[1024]{0:T(1024)S(1)}, f32[1024]{0:T(1024)}, u32[]{:S(2)}) copy-start(f32[1024]{0:T(1024)} %param.21) | copy-start | bytes 12292
where the time goes:
time: 191 us; the launch traced here: 189 us
  waiting for transfers between devices  71.9 us (38%)
  local copies, waits for them, and re-layouts  54 us (28%)
  starting transfers between devices  35.3 us (18%)
  blocking collectives  13.5 us (7%)
  other arithmetic  7.97 us (4%)
  matrix products  6.56 us (3%)
    all_to_all x1, waiting for transfers between devices, per_device(): lax.all_to_all(packed_keys, 'rep', split_axis=0, concat_axis=0, tiled=True)  53.6 us
    scatter x1, local copies, waits for them, and re-layouts, per_device(): key_pool.at[incoming]  17.5 us
    all_to_all x1, waiting for transfers between devices, per_device(): lax.all_to_all(packed_values, 'rep', split_axis=0, concat_axis=0, tiled=T...  17.1 us
    all_to_all x1, starting transfers between devices, per_device(): lax.all_to_all(notice.reshape(replicas, CAP), 'rep', split_axis=0, concat...  15.4 us
    psum x1, blocking collectives, per_device(): squares = lax.psum(jnp.sum(attention * attention, axis=-1), 'tp')  13.5 us
    scatter x1, local copies, waits for them, and re-layouts, per_device(): value_pool.at[incoming]  12 us
    all_to_all x1, starting transfers between devices, per_device(): lax.all_to_all(packed_keys, 'rep', split_axis=0, concat_axis=0, tiled=True)  11.7 us
    all_to_all x1, starting transfers between devices, per_device(): lax.all_to_all(packed_values, 'rep', split_axis=0, concat_axis=0, tiled=T...  8.25 us
  transfers between devices with their start and end apart: 3, of which 3 were waited for; matrix products, arithmetic and copies ran while one was open for 24% of the time, Pallas kernels for 0%

commit v1 on v0

v1 whole, which is shorter than its diff:
```python
import functools
import math

import jax
import jax.numpy as jnp
from jax import lax
from jax.experimental import pallas as pl
from jax.experimental.pallas import tpu as pltpu
from jax.sharding import PartitionSpec as P

HD = 128
MASKED = -1e30
HUGE = 3e38
TOP = 32767.0
MESH = pl.DeviceIdType.MESH
I32 = jnp.int32
F32 = jnp.float32
BF16 = jnp.bfloat16


def iota(shape, dim):
    return lax.broadcasted_iota(I32, shape, dim)


def to_column(row, size):
    shape = (size, size)
    return jnp.sum(jnp.where(iota(shape, 0) == iota(shape, 1), row, 0.0), axis=1, keepdims=True)


def to_row(column, size):
    shape = (size, size)
    return jnp.sum(jnp.where(iota(shape, 0) == iota(shape, 1), column, 0.0), axis=0, keepdims=True)


def block_sums(queries, keys, values, caps):
    scores = lax.dot_general(queries, keys, (((1,), (1,)), ((), ())), preferred_element_type=F32)
    scores = jnp.minimum(scores * (1.0 / math.sqrt(HD)), caps)
    maxima = jnp.max(scores, axis=1, keepdims=True)
    weights = jnp.exp(scores - maxima)
    totals = jnp.sum(weights, axis=1, keepdims=True)
    sums = jnp.dot(weights.astype(BF16), values, preferred_element_type=F32)
    return maxima, totals, sums


def kernel(
    n, nz, tp,
    table_s, context_s,
    q_ref, nk_ref, nv_ref, kp_ref, vp_ref, table_ref, context_ref, source_ref, replica_ref, target_ref, gain_ref,
    out_ref,
    kv, vv, qf, qb, nk, nv,
    note_out, note_in, lists, lists_s, caps,
    q_out, q_in, sum_out, sum_in, stat_out, stat_in,
    near, near_log, draft, draft_log, attention, squares, scales, norm_rows,
    pool_sem, list_sem, note_send, note_recv, q_send, q_recv, sum_send, sum_recv, stat_send, stat_recv, norm_send, norm_recv,
):
    ny = n // nz
    requests, steps, width = q_ref.shape
    heads = width // HD
    rows = steps * heads
    entries = replica_ref.shape[1]
    slots = kp_ref.shape[0]
    page = kp_ref.shape[1]
    me = lax.axis_index("rep")
    lane_me = lax.axis_index("tp")
    my, mz = lax.div(me, nz), lax.rem(me, nz)

    def ahead(q):
        return lax.rem(my + lax.div(q, nz), ny) * nz + lax.rem(mz + lax.rem(q, nz), nz)

    def behind(q):
        return lax.rem(my + ny - lax.div(q, nz), ny) * nz + lax.rem(mz + nz - lax.rem(q, nz), nz)

    def opposite(q):
        return lax.rem(ny - lax.div(q, nz), ny) * nz + lax.rem(nz - lax.rem(q, nz), nz)

    def order(step):
        return lax.rem((step + 1) * 27, n)

    barrier = pltpu.get_barrier_semaphore()

    def greet(step, carry):
        pl.semaphore_signal(barrier, inc=1, device_id=(ahead(step + 1), lane_me), device_id_type=MESH)
        return carry

    lax.fori_loop(0, n - 1, greet, 0)
    for other in range(1, tp):
        pl.semaphore_signal(barrier, inc=1, device_id=(me, lax.rem(lane_me + other, tp)), device_id_type=MESH)

    pool_copies = [
        pltpu.make_async_copy(kp_ref, kv, pool_sem.at[0]),
        pltpu.make_async_copy(vp_ref, vv, pool_sem.at[1]),
    ]
    for copy in pool_copies:
        copy.start()

    replica = replica_ref[...].astype(F32)
    source = source_ref[...].astype(F32)
    target = target_ref[...].astype(F32)
    square = (entries, entries)
    replica_c = to_column(replica, entries)
    same_before = (replica_c == replica) & (iota(square, 0) < iota(square, 1))
    rank = jnp.sum(jnp.where(same_before, 1.0, 0.0), axis=0, keepdims=True)
    rank_c = to_column(rank, entries)
    source_c = to_column(source, entries)

    def vector_peer(q, sign):
        dy, dz = q // nz, q % nz
        return (((my + ny + sign * dy) % ny) * nz + (mz + nz + sign * dz) % nz).astype(F32)

    def targets_of(sign):
        peers = vector_peer(iota((n, entries), 0), sign)
        found = []
        for k in range(2):
            chosen = (peers == replica) & (rank == float(k))
            found.append(jnp.sum(jnp.where(chosen, target + 1.0, 0.0), axis=1, keepdims=True) - 1.0)
        return found

    wide = (entries, 2 * n)
    peers_row = vector_peer(iota(wide, 1) % n, 1)
    chosen = (replica_c == peers_row) & (rank_c == (iota(wide, 1) // n).astype(F32))
    source_row = jnp.sum(jnp.where(chosen, source_c, 0.0), axis=0, keepdims=True)

    context_c = to_column(context_ref[...].astype(F32), requests)
    by_slot = (requests, slots)
    slot_lane = iota(by_slot, 1).astype(F32)
    request_c = iota(by_slot, 0).astype(F32)
    valid_row = jnp.zeros((1, slots), F32)
    place_row = jnp.zeros((1, slots), F32)
    for p in range(2):
        table_c = to_column(table_ref[p : p + 1, :].astype(F32), requests)
        here = table_c == slot_lane
        valid = jnp.clip(context_c - float(p * page), 0.0, float(page))
        valid_row += jnp.sum(jnp.where(here, valid, 0.0), axis=0, keepdims=True)
        place_row += jnp.sum(jnp.where(here, request_c + float(p * requests), 0.0), axis=0, keepdims=True)

    notes = (n, slots)
    lane = iota(notes, 1).astype(F32)
    first, second = targets_of(1)
    marks = jnp.where(lane == first, 65536.0, 0.0) + jnp.where(lane == second, 131072.0, 0.0)
    code = (valid_row + marks).astype(I32)
    for q in range(n):
        note_out[q] = code[q : q + 1, :]
    first_back, second_back = targets_of(-1)
    note_in[0] = jnp.zeros((1, slots), I32)
    sum_in[pl.ds(0, 2)] = jnp.zeros((2, rows, HD), jnp.int16)
    stat_in[0] = jnp.zeros((1, 2 * 2 * rows), F32)

    pl.semaphore_wait(barrier, n - 1 + tp - 1)

    def note_copy(q):
        return pltpu.make_async_remote_copy(
            src_ref=note_out.at[q], dst_ref=note_in.at[q], send_sem=note_send, recv_sem=note_recv,
            device_id=(ahead(q), lane_me), device_id_type=MESH,
        )

    def send_note(step, carry):
        note_copy(order(step)).start()
        return carry

    lax.fori_loop(0, n - 1, send_note, 0)

    def spread(i, carry):
        for h in range(heads):
            qf[pl.ds(i * rows + h, steps, stride=heads), :] = q_ref[i, :, h * HD : (h + 1) * HD].astype(F32)
        return carry

    lax.fori_loop(0, requests, spread, 0)

    def narrow(i, carry):
        qb[i] = qf[pl.ds(pl.multiple_of(i * rows, rows), rows), :].astype(BF16)
        return carry

    lax.fori_loop(0, requests, narrow, 0)

    def wait_all(buffer, sem, count):
        pltpu.make_async_copy(buffer.at[pl.ds(1, count)], buffer.at[pl.ds(1, count)], sem).wait()

    wait_all(note_in, note_recv, n - 1)

    got = note_in[...].reshape(n, slots)
    mark = got >> 16
    count = (got & 65535).astype(F32)
    place_0 = jnp.sum(jnp.where(mark == 1, place_row + 1.0, 0.0), axis=1, keepdims=True) - 1.0
    place_1 = jnp.sum(jnp.where(mark == 2, place_row + 1.0, 0.0), axis=1, keepdims=True) - 1.0
    valid_0 = jnp.sum(jnp.where(lane == first_back, count, 0.0), axis=1, keepdims=True)
    valid_1 = jnp.sum(jnp.where(lane == second_back, count, 0.0), axis=1, keepdims=True)
    caps[0, 0:n] = jnp.where(lane < valid_0, HUGE, MASKED)
    caps[1, 0:n] = jnp.where((lane >= float(page)) & (lane < valid_1 + float(page)), HUGE, MASKED)

    line = (n, 2 * n)
    lane_2 = iota(line, 1)
    distance = iota(line, 0)
    request_0 = jnp.maximum(place_0, 0.0) - jnp.where(place_0 >= float(requests), float(requests), 0.0)
    request_1 = jnp.maximum(place_1, 0.0) - jnp.where(place_1 >= float(requests), float(requests), 0.0)
    request_row = jnp.sum(
        jnp.where(lane_2 == distance, request_0, 0.0) + jnp.where(lane_2 == distance + n, request_1, 0.0),
        axis=0, keepdims=True,
    )
    by_place = (n, HD)
    place_lane = iota(by_place, 1).astype(F32)
    distance_2 = 2.0 * iota(by_place, 0).astype(F32)
    origin_row = jnp.sum(
        jnp.where(place_lane == place_0, distance_2 + 1.0, 0.0) + jnp.where(place_lane == place_1, distance_2 + 2.0, 0.0),
        axis=0, keepdims=True,
    )
    lists[...] = jnp.zeros(lists.shape, I32)
    lists[0:1, 0 : 2 * n] = source_row.astype(I32)
    lists[1:2, 0 : 2 * n] = request_row.astype(I32)
    lists[2:3, :] = origin_row.astype(I32)
    list_copy = pltpu.make_async_copy(lists, lists_s, list_sem)
    list_copy.start()
    list_copy.wait()

    def listed(line, at, limit):
        return jnp.minimum(jnp.maximum(lists_s[line, at], 0), limit)

    def q_copy(q):
        return pltpu.make_async_remote_copy(
            src_ref=q_out.at[q], dst_ref=q_in.at[q], send_sem=q_send, recv_sem=q_recv.at[q],
            device_id=(behind(q), lane_me), device_id_type=MESH,
        )

    def send_queries(step, carry):
        q = order(step)
        q_out[q, 0:rows] = qb[listed(1, q, requests - 1)]
        q_out[q, rows : 2 * rows] = qb[listed(1, q + n, requests - 1)]
        q_copy(q).start()
        return carry

    lax.fori_loop(0, n - 1, send_queries, 0)

    for copy in pool_copies:
        copy.wait()
    tall = (2 * rows, HD)
    upper = iota(tall, 0) < rows
    key_lane = iota(tall, 1)

    def own_pages(i, carry):
        context = context_s[i]
        limit_0 = jnp.minimum(context, page)
        allowed = (upper & (key_lane < limit_0)) | ((~upper) & (key_lane >= page) & (key_lane < context))
        pages = (table_s[0, i], table_s[1, i])
        mine = qb[i]
        maxima, totals, sums = block_sums(
            jnp.concatenate([mine, mine], axis=0),
            jnp.concatenate([kv[pages[0]], kv[pages[1]]], axis=0),
            jnp.concatenate([vv[pages[0]], vv[pages[1]]], axis=0),
            jnp.where(allowed, HUGE, MASKED),
        )
        near[i] = sums / totals
        near_log[i] = jnp.broadcast_to(maxima + jnp.log(totals), tall)
        return carry

    lax.fori_loop(0, requests, own_pages, 0)

    for i in range(requests):
        nk[i * steps : (i + 1) * steps, :] = nk_ref[i].astype(F32)
        nv[i * steps : (i + 1) * steps, :] = nv_ref[i].astype(F32)
    draft_keys = nk[...].astype(BF16)
    draft_values = nv[...].astype(BF16)
    chunk = HD // rows
    blocky = (HD, HD)
    key_at = iota(blocky, 1)
    row_at = iota(blocky, 0)

    def own_draft(c, carry):
        request = c * chunk + row_at // rows
        allowed = (key_at // steps == request) & (key_at % steps <= (row_at % rows) // heads)
        block = qb[pl.ds(c * chunk, chunk)].reshape(HD, HD)
        maxima, totals, sums = block_sums(block, draft_keys, draft_values, jnp.where(allowed, HUGE, MASKED))
        at = pl.ds(pl.multiple_of(c * HD, HD), HD)
        draft[at, :] = sums / totals
        draft_log[at, :] = jnp.broadcast_to(maxima + jnp.log(totals), blocky)
        return carry

    lax.fori_loop(0, requests // chunk, own_draft, 0)

    def sum_copy(q):
        return pltpu.make_async_remote_copy(
            src_ref=sum_out.at[pl.ds(2 * q, 2)], dst_ref=sum_in.at[pl.ds(2 * q, 2)], send_sem=sum_send, recv_sem=sum_recv,
            device_id=(ahead(q), lane_me), device_id_type=MESH,
        )

    def stat_copy(q):
        return pltpu.make_async_remote_copy(
            src_ref=stat_out.at[q], dst_ref=stat_in.at[q], send_sem=stat_send, recv_sem=stat_recv,
            device_id=(ahead(q), lane_me), device_id_type=MESH,
        )

    stat_row = iota(tall, 0)

    def serve(step, carry):
        q = order(step)
        back = opposite(q)
        q_copy(q).wait_recv()
        pages = (listed(0, q, slots - 1), listed(0, q + n, slots - 1))
        cap = jnp.where(upper, caps[0, pl.ds(back, 1), :], caps[1, pl.ds(back, 1), :])
        maxima, totals, sums = block_sums(
            q_in[q],
            jnp.concatenate([kv[pages[0]], kv[pages[1]]], axis=0),
            jnp.concatenate([vv[pages[0]], vv[pages[1]]], axis=0),
            cap,
        )
        largest = jnp.maximum(jnp.max(jnp.abs(sums), axis=1, keepdims=True), 1e-30)
        coded = jnp.round(sums * (TOP / largest)).astype(I32).astype(jnp.int16)
        sum_out[2 * q] = coded[0:rows]
        sum_out[2 * q + 1] = coded[rows : 2 * rows]
        logs = maxima + jnp.log(totals)
        factor = largest / (TOP * totals)
        stat_out[q] = jnp.sum(
            jnp.where(key_lane == stat_row, logs, 0.0) + jnp.where(key_lane == stat_row + 2 * rows, factor, 0.0),
            axis=0, keepdims=True,
        )
        sum_copy(q).start()
        stat_copy(q).start()
        return carry

    lax.fori_loop(0, n - 1, serve, 0)

    def wait_sums(buffer, sem):
        view = buffer.at[pl.ds(2, 2 * n - 2)]
        pltpu.make_async_copy(view, view, sem).wait()

    wait_sums(sum_in, sum_recv)
    wait_all(stat_in, stat_recv, n - 1)

    short = (rows, HD)
    skew = iota(short, 1) - iota(short, 0)

    def combine(i, carry):
        means, logs = [], []
        for p in range(2):
            origin = listed(2, p * requests + i, 2 * n)
            away = jnp.maximum(origin - 1, 0)
            k = lax.rem(away, 2)
            stats = stat_in[lax.div(away, 2)]
            log = jnp.sum(jnp.where(skew == k * rows, stats, 0.0), axis=1, keepdims=True)
            factor = jnp.sum(jnp.where(skew == (k + 2) * rows, stats, 0.0), axis=1, keepdims=True)
            mean = sum_in[away].astype(F32) * factor
            at = pl.ds(p * rows, rows)
            means.append(jnp.where(origin > 0, mean, near[i, at]))
            logs.append(jnp.where(origin > 0, log, near_log[i, at]))
        at = pl.ds(pl.multiple_of(i * rows, rows), rows)
        means.append(draft[at, :])
        logs.append(draft_log[at, :])
        largest = jnp.maximum(jnp.maximum(logs[0], logs[1]), logs[2])
        factors = [jnp.exp(log - largest) for log in logs]
        numerator = factors[0] * means[0] + factors[1] * means[1] + factors[2] * means[2]
        result = numerator / (factors[0] + factors[1] + factors[2])
        attention[at, :] = result
        squares[i] = jnp.sum((result * result).reshape(steps, heads, HD), axis=1)
        return carry

    lax.fori_loop(0, requests, combine, 0)

    tokens = requests * steps
    total_c = jnp.sum(squares[...].reshape(tokens, HD), axis=1, keepdims=True)
    norm_rows[0] = to_row(total_c, tokens)

    def norm_copy(other):
        return pltpu.make_async_remote_copy(
            src_ref=norm_rows.at[0], dst_ref=norm_rows.at[other], send_sem=norm_send.at[other], recv_sem=norm_recv.at[other],
            device_id=(me, lax.rem(lane_me + other, tp)), device_id_type=MESH,
        )

    for other in range(1, tp):
        norm_copy(other).start()
    for other in range(1, tp):
        norm_copy(other).wait_recv()
    total = norm_rows[0]
    for other in range(1, tp):
        total = total + norm_rows[other]
    scale = lax.rsqrt(total * (1.0 / (tp * width)) + 1e-05)
    scales[...] = jnp.broadcast_to(to_column(scale, tokens), (tokens, HD)).reshape(requests, steps, HD)

    def finish(i, carry):
        for h in range(heads):
            at = slice(h * HD, (h + 1) * HD)
            out_ref[i, :, at] = attention[pl.ds(i * rows + h, steps, stride=heads), :] * scales[i] * gain_ref[:, at]
        return carry

    lax.fori_loop(0, requests, finish, 0)

    for other in range(1, tp):
        norm_copy(other).wait_send()
    wait_all(note_out, note_send, n - 1)
    wait_all(q_out, q_send, n - 1)
    wait_sums(sum_out, sum_send)
    wait_all(stat_out, stat_send, n - 1)


def per_device(n, nz, tp, queries, new_keys, new_values, key_pool, value_pool, block_table, context, source, replica, target, gain):
    requests, steps, width = queries.shape
    rows = steps * width // HD
    slots, page, _ = key_pool.shape
    entries = source.shape[0]
    vmem = pl.BlockSpec(memory_space=pltpu.VMEM)
    smem = pl.BlockSpec(memory_space=pltpu.SMEM)
    anywhere = pl.BlockSpec(memory_space=pl.ANY)
    dma = pltpu.SemaphoreType.DMA
    table = block_table.T
    return pl.pallas_call(
        functools.partial(kernel, n, nz, tp),
        out_shape=jax.ShapeDtypeStruct((requests, steps, width), F32),
        in_specs=[smem, smem, vmem, vmem, vmem, anywhere, anywhere] + [vmem] * 6,
        out_specs=vmem,
        scratch_shapes=[
            pltpu.VMEM((slots, page, HD), BF16),
            pltpu.VMEM((slots, page, HD), BF16),
            pltpu.VMEM(((requests + 1) * rows, HD), F32),
            pltpu.VMEM((requests, rows, HD), BF16),
            pltpu.VMEM((requests * steps, HD), F32),
            pltpu.VMEM((requests * steps, HD), F32),
            pltpu.VMEM((n, 1, slots), I32),
            pltpu.VMEM((n, 1, slots), I32),
            pltpu.VMEM((8, HD), I32),
            pltpu.SMEM((8, HD), I32),
            pltpu.VMEM((2, n + 8, slots), F32),
            pltpu.VMEM((n, 2 * rows, HD), BF16),
            pltpu.VMEM((n, 2 * rows, HD), BF16),
            pltpu.VMEM((2 * n, rows, HD), jnp.int16),
            pltpu.VMEM((2 * n, rows, HD), jnp.int16),
            pltpu.VMEM((n, 1, HD), F32),
            pltpu.VMEM((n, 1, HD), F32),
            pltpu.VMEM((requests, 2 * rows, HD), F32),
            pltpu.VMEM((requests, 2 * rows, HD), F32),
            pltpu.VMEM((requests * rows, HD), F32),
            pltpu.VMEM((requests * rows, HD), F32),
            pltpu.VMEM(((requests + 1) * rows, HD), F32),
            pltpu.VMEM((requests, steps, HD), F32),
            pltpu.VMEM((requests, steps, HD), F32),
            pltpu.VMEM((tp, 1, HD), F32),
            dma((2,)), dma, dma, dma, dma, dma((n,)), dma, dma, dma, dma, dma((tp,)), dma((tp,)),
        ],
        compiler_params=pltpu.CompilerParams(collective_id=0, has_side_effects=True, vmem_limit_bytes=40 * 2**20),
    )(
        table, context, queries, new_keys, new_values, key_pool, value_pool, table,
        context.reshape(1, requests), source.reshape(1, entries), replica.reshape(1, entries), target.reshape(1, entries),
        gain.reshape(1, width),
    )


def solution(mesh):
    n, tp = mesh.shape["rep"], mesh.shape["tp"]
    nz = 2 ** (n.bit_length() // 2)
    heads, replicas = P("rep", None, "tp"), P("rep")
    return jax.shard_map(
        functools.partial(per_device, n, nz, tp),
        mesh=mesh,
        in_specs=(heads, heads, heads, heads, heads, P("rep", None), replicas, replicas, replicas, replicas, P("tp")),
        out_specs=heads,
        check_vma=False,
    )
```

time: 191 us -> 97.7 us (0.51)
  the two profiles are of different devices: /device:TPU:104 before, /device:TPU:1 now
where the time goes in v1:
time: 97.7 us; the launch traced here: 97.2 us
  Pallas kernels  86.8 us (89%)
  local copies, waits for them, and re-layouts  10.4 us (11%)
    pallas_call x1, Pallas kernels, per_device(): pl.pallas_call(functools.partial(kernel, n, nz, tp), out_shape=jax.ShapeD...  86.8 us
    unnamed x23, local copies, waits for them, and re-layouts  10.4 us

profile of v1, /device:TPU:1, one launch (start us, length us, event | category | flops | bytes accessed | tf_op | source)
XLA Modules:
  0.0 97.2 jit_solution(15918085635355535462)
XLA Ops:
  0.0 0.0 copy-start
  0.0 1.6 %copy-done = bf16[128,64,128]{2,1,0:T(8,128)(2,1)S(1)} copy-done((bf16[128,64,128]{2,1,0:T(8,128)(2,1)S(1)}, bf16[128,64,128]{2,1,0:T(8,128)(2,1)}, u32[]{:S(2)}) %copy-start) | copy-done | bytes 2097176
  1.6 0.0 copy-start.1
  1.6 1.6 %copy-done.1 = bf16[128,64,128]{2,1,0:T(8,128)(2,1)S(1)} copy-done((bf16[128,64,128]{2,1,0:T(8,128)(2,1)S(1)}, bf16[128,64,128]{2,1,0:T(8,128)(2,1)}, u32[]{:S(2)}) %copy-start.1) | copy-done | bytes 2097176
  3.2 0.0 copy-start.2
  3.2 0.9 copy-done.2
  4.1 0.0 copy-start.3
  4.1 0.8 copy-done.3
  4.9 0.0 copy-start.4
  4.9 0.8 copy-done.4
  5.7 0.0 copy-start.5
  5.7 0.7 copy-done.5
  6.3 0.0 copy-start.6
  6.3 0.7 copy-done.6
  7.0 0.0 copy-start.7
  7.0 0.7 copy-done.7
  7.7 0.0 copy-start.8
  7.7 0.7 copy-done.8
  8.3 0.0 copy-start.9
  8.3 0.7 copy-done.9
  9.0 0.0 copy-start.10
  9.0 0.7 copy-done.10
  9.6 86.8 %shard_map.109 = f32[32,4,1024]{2,1,0:T(4,128)S(1)} custom-call(s32[2,32]{1,0:T(2,128)S(1)} %bitcast.7, s32[32]{0:T(128)S(1)} %copy-done.7, bf16[32,4,1024]{2,1,0:T(4,128)(2,1)S(1)} %copy-done.2, bf16[32,4,128]{2,1,0:T(4,128)(2,1)S(1)} %copy-done.3, bf16[32,4,128]{2,1,0:T(4,128)(2,1)S(1)} %copy-done.4, bf16[128,64,128]{2,1,0:T(8,128)(2,1)S(1)} %copy-done, ...), custom_call_target="tpu_custom_call" | custom-call | tf_op jit(solution)/shard_map/pallas_call | solution.py:402
  96.4 0.8 copy.13
Async XLA Ops:
  0.0 1.6 %copy-start = (bf16[128,64,128]{2,1,0:T(8,128)(2,1)S(1)}, bf16[128,64,128]{2,1,0:T(8,128)(2,1)}, u32[]{:S(2)}) copy-start(bf16[128,64,128]{2,1,0:T(8,128)(2,1)} %kp_ref.1) | copy-start | bytes 6291460
  1.6 1.6 %copy-start.1 = (bf16[128,64,128]{2,1,0:T(8,128)(2,1)S(1)}, bf16[128,64,128]{2,1,0:T(8,128)(2,1)}, u32[]{:S(2)}) copy-start(bf16[128,64,128]{2,1,0:T(8,128)(2,1)} %vp_ref.1) | copy-start | bytes 6291460
  3.2 0.9 copy-start.2
  4.1 0.8 copy-start.3
  4.9 0.8 copy-start.4
  5.7 0.7 copy-start.5
  6.3 0.7 copy-start.6
  7.0 0.7 copy-start.7
  7.7 0.7 copy-start.8
  8.3 0.7 copy-start.9
  9.0 0.7 copy-start.10

commit v2 on v1

--- a/solution.py
+++ b/solution.py
@@ -12,6 +12,9 @@
 MASKED = -1e30
 HUGE = 3e38
 TOP = 32767.0
+OWN = 4
+SERVE = 4
+COMBINE = 4
 MESH = pl.DeviceIdType.MESH
 I32 = jnp.int32
 F32 = jnp.float32
@@ -30,6 +33,28 @@
 def to_row(column, size):
     shape = (size, size)
     return jnp.sum(jnp.where(iota(shape, 0) == iota(shape, 1), column, 0.0), axis=0, keepdims=True)
+
+
+def column_sums(queries, keys, values, limit):
+    page = keys[0].shape[0]
+    rows = HD // len(keys)
+    shape = (page, HD)
+    slot = iota(shape, 1) // rows
+    products = [
+        lax.dot_general(key, queries, (((1,), (1,)), ((), ())), preferred_element_type=F32) for key in keys
+    ]
+    scores = products[0]
+    for b in range(1, len(keys)):
+        scores = jnp.where(slot == b, products[b], scores)
+    scores = jnp.where(iota(shape, 0).astype(F32) < limit, scores * (1.0 / math.sqrt(HD)), MASKED)
+    maxima = jnp.max(scores, axis=0, keepdims=True)
+    weights = jnp.exp(scores - maxima)
+    totals = jnp.sum(weights, axis=0, keepdims=True)
+    turned = weights.T.astype(BF16)
+    sums = [
+        jnp.dot(turned[b * rows : (b + 1) * rows], values[b], preferred_element_type=F32) for b in range(len(keys))
+    ]
+    return maxima, totals, jnp.concatenate(sums, axis=0)
 
 
 def block_sums(queries, keys, values, caps):
@@ -44,20 +69,20 @@
 
 def kernel(
     n, nz, tp,
-    table_s, context_s,
-    q_ref, nk_ref, nv_ref, kp_ref, vp_ref, table_ref, context_ref, source_ref, replica_ref, target_ref, gain_ref,
+    q_hbm, nk_hbm, nv_hbm, kp_ref, vp_ref, table_hbm, context_hbm, source_hbm, replica_hbm, target_hbm, gain_hbm,
     out_ref,
+    table_s, context_s, q_ref, nk_ref, nv_ref, table_ref, context_ref, source_ref, replica_ref, target_ref, gain_ref,
     kv, vv, qf, qb, nk, nv,
-    note_out, note_in, lists, lists_s, caps,
+    note_out, note_in, lists, lists_s, limits,
     q_out, q_in, sum_out, sum_in, stat_out, stat_in,
-    near, near_log, draft, draft_log, attention, squares, scales, norm_rows,
-    pool_sem, list_sem, note_send, note_recv, q_send, q_recv, sum_send, sum_recv, stat_send, stat_recv, norm_send, norm_recv,
+    near, near_stat, draft, draft_log, attention, squares, scales, norm_rows,
+    in_sem, list_sem, note_send, note_recv, q_send, q_recv, sum_send, sum_recv, stat_send, stat_recv, norm_send, norm_recv,
 ):
     ny = n // nz
-    requests, steps, width = q_ref.shape
+    requests, steps, width = q_hbm.shape
     heads = width // HD
     rows = steps * heads
-    entries = replica_ref.shape[1]
+    entries = replica_hbm.shape[1]
     slots = kp_ref.shape[0]
     page = kp_ref.shape[1]
     me = lax.axis_index("rep")
@@ -76,6 +101,15 @@
     def order(step):
         return lax.rem((step + 1) * 27, n)
 
+    moves = [
+        (replica_hbm, replica_ref), (source_hbm, source_ref), (target_hbm, target_ref), (table_hbm, table_ref),
+        (context_hbm, context_ref), (q_hbm, q_ref), (table_hbm, table_s), (context_hbm, context_s), (nk_hbm, nk_ref),
+        (nv_hbm, nv_ref), (kp_ref, kv), (vp_ref, vv), (gain_hbm, gain_ref),
+    ]
+    fetches = [pltpu.make_async_copy(a, b, in_sem.at[at]) for at, (a, b) in enumerate(moves)]
+    for fetch in fetches:
+        fetch.start()
+
     barrier = pltpu.get_barrier_semaphore()
 
     def greet(step, carry):
@@ -86,12 +120,8 @@
     for other in range(1, tp):
         pl.semaphore_signal(barrier, inc=1, device_id=(me, lax.rem(lane_me + other, tp)), device_id_type=MESH)
 
-    pool_copies = [
-        pltpu.make_async_copy(kp_ref, kv, pool_sem.at[0]),
-        pltpu.make_async_copy(vp_ref, vv, pool_sem.at[1]),
-    ]
-    for copy in pool_copies:
-        copy.start()
+    for fetch in fetches[0:5]:
+        fetch.wait()
 
     replica = replica_ref[...].astype(F32)
     source = source_ref[...].astype(F32)
@@ -142,6 +172,7 @@
         note_out[q] = code[q : q + 1, :]
     first_back, second_back = targets_of(-1)
     note_in[0] = jnp.zeros((1, slots), I32)
+    q_in[0] = jnp.zeros((2 * rows, HD), BF16)
     sum_in[pl.ds(0, 2)] = jnp.zeros((2, rows, HD), jnp.int16)
     stat_in[0] = jnp.zeros((1, 2 * 2 * rows), F32)
 
@@ -158,6 +189,8 @@
         return carry
 
     lax.fori_loop(0, n - 1, send_note, 0)
+
+    fetches[5].wait()
 
     def spread(i, carry):
         for h in range(heads):
@@ -184,8 +217,8 @@
     place_1 = jnp.sum(jnp.where(mark == 2, place_row + 1.0, 0.0), axis=1, keepdims=True) - 1.0
     valid_0 = jnp.sum(jnp.where(lane == first_back, count, 0.0), axis=1, keepdims=True)
     valid_1 = jnp.sum(jnp.where(lane == second_back, count, 0.0), axis=1, keepdims=True)
-    caps[0, 0:n] = jnp.where(lane < valid_0, HUGE, MASKED)
-    caps[1, 0:n] = jnp.where((lane >= float(page)) & (lane < valid_1 + float(page)), HUGE, MASKED)
+    half = lane - jnp.where(lane >= float(2 * rows), float(2 * rows), 0.0)
+    limits[0:n] = jnp.where(half < float(rows), valid_0, valid_1)
 
     line = (n, 2 * n)
     lane_2 = iota(line, 1)
@@ -229,29 +262,35 @@
 
     lax.fori_loop(0, n - 1, send_queries, 0)
 
-    for copy in pool_copies:
-        copy.wait()
-    tall = (2 * rows, HD)
-    upper = iota(tall, 0) < rows
-    key_lane = iota(tall, 1)
-
-    def own_pages(i, carry):
-        context = context_s[i]
-        limit_0 = jnp.minimum(context, page)
-        allowed = (upper & (key_lane < limit_0)) | ((~upper) & (key_lane >= page) & (key_lane < context))
-        pages = (table_s[0, i], table_s[1, i])
-        mine = qb[i]
-        maxima, totals, sums = block_sums(
-            jnp.concatenate([mine, mine], axis=0),
-            jnp.concatenate([kv[pages[0]], kv[pages[1]]], axis=0),
-            jnp.concatenate([vv[pages[0]], vv[pages[1]]], axis=0),
-            jnp.where(allowed, HUGE, MASKED),
-        )
-        near[i] = sums / totals
-        near_log[i] = jnp.broadcast_to(maxima + jnp.log(totals), tall)
-        return carry
-
-    lax.fori_loop(0, requests, own_pages, 0)
+    for fetch in fetches[6:]:
+        fetch.wait()
+    lane_1 = iota((1, HD), 1)
+    own_lane = lane_1 // rows
+
+    def stat_pair(logs, factors):
+        low = lane_1 < 2 * rows
+        return (
+            jnp.where(low, logs, pltpu.roll(factors, 2 * rows, axis=1)),
+            jnp.where(low, pltpu.roll(logs, 2 * rows, axis=1), factors),
+        )
+
+    def own_pages(step, carry):
+        pair = (2 * step, 2 * step + 1)
+        first_context, second_context = context_s[0, pair[0]], context_s[0, pair[1]]
+        limit = jnp.where(own_lane < 2, first_context, second_context) - jnp.where(own_lane % 2 == 1, page, 0)
+        pages = [table_s[p, i] for i in pair for p in range(2)]
+        mine = [qb[i] for i in pair]
+        maxima, totals, sums = column_sums(
+            jnp.concatenate([mine[0], mine[0], mine[1], mine[1]], axis=0),
+            [kv[at] for at in pages], [vv[at] for at in pages], limit.astype(F32),
+        )
+        stats = stat_pair(maxima + jnp.log(totals), 1.0 / totals)
+        for at, i in enumerate(pair):
+            near[i] = sums[at * 2 * rows : (at + 1) * 2 * rows]
+            near_stat[i] = stats[at]
+        return carry
+
+    lax.fori_loop(0, requests // 2, own_pages, 0, unroll=OWN)
 
     for i in range(requests):
         nk[i * steps : (i + 1) * steps, :] = nk_ref[i].astype(F32)
@@ -273,7 +312,7 @@
         draft_log[at, :] = jnp.broadcast_to(maxima + jnp.log(totals), blocky)
         return carry
 
-    lax.fori_loop(0, requests // chunk, own_draft, 0)
+    lax.fori_loop(0, requests // chunk, own_draft, 0, unroll=2)
 
     def sum_copy(q):
         return pltpu.make_async_remote_copy(
@@ -287,35 +326,45 @@
             device_id=(ahead(q), lane_me), device_id_type=MESH,
         )
 
-    stat_row = iota(tall, 0)
-
-    def serve(step, carry):
-        q = order(step)
-        back = opposite(q)
-        q_copy(q).wait_recv()
-        pages = (listed(0, q, slots - 1), listed(0, q + n, slots - 1))
-        cap = jnp.where(upper, caps[0, pl.ds(back, 1), :], caps[1, pl.ds(back, 1), :])
-        maxima, totals, sums = block_sums(
-            q_in[q],
-            jnp.concatenate([kv[pages[0]], kv[pages[1]]], axis=0),
-            jnp.concatenate([vv[pages[0]], vv[pages[1]]], axis=0),
-            cap,
+    square_1 = iota(blocky, 0) == iota(blocky, 1)
+
+    def serve_pair(first_q, second_q):
+        pair = (first_q, second_q)
+        pages = [listed(0, q + k * n, slots - 1) for q in pair for k in range(2)]
+        ends = [limits[pl.ds(opposite(q), 1), :] for q in pair]
+        maxima, totals, sums = column_sums(
+            jnp.concatenate([q_in[q] for q in pair], axis=0),
+            [kv[at] for at in pages], [vv[at] for at in pages], jnp.where(own_lane < 2, ends[0], ends[1]),
         )
         largest = jnp.maximum(jnp.max(jnp.abs(sums), axis=1, keepdims=True), 1e-30)
         coded = jnp.round(sums * (TOP / largest)).astype(I32).astype(jnp.int16)
-        sum_out[2 * q] = coded[0:rows]
-        sum_out[2 * q + 1] = coded[rows : 2 * rows]
-        logs = maxima + jnp.log(totals)
-        factor = largest / (TOP * totals)
-        stat_out[q] = jnp.sum(
-            jnp.where(key_lane == stat_row, logs, 0.0) + jnp.where(key_lane == stat_row + 2 * rows, factor, 0.0),
-            axis=0, keepdims=True,
-        )
+        largest_row = jnp.sum(jnp.where(square_1, largest, 0.0), axis=0, keepdims=True)
+        stats = stat_pair(maxima + jnp.log(totals), largest_row / (TOP * totals))
+        for at, q in enumerate(pair):
+            sum_out[pl.ds(2 * q, 2)] = coded[at * 2 * rows : (at + 1) * 2 * rows].reshape(2, rows, HD)
+            stat_out[q] = stats[at]
+
+    def serve(step, carry):
+        qs = [order(step * SERVE + at) for at in range(SERVE)]
+        for q in qs:
+            q_copy(q).wait_recv()
+        for at in range(0, SERVE, 2):
+            serve_pair(qs[at], qs[at + 1])
+        for q in qs:
+            sum_copy(q).start()
+            stat_copy(q).start()
+        return carry
+
+    whole = (n - 2) // SERVE
+    lax.fori_loop(0, whole, serve, 0)
+    rest = [order(step) for step in range(whole * SERVE, n - 1)]
+    for q in rest:
+        q_copy(q).wait_recv()
+    for at in range(0, len(rest), 2):
+        serve_pair(rest[at], rest[at + 1] if at + 1 < len(rest) else 0)
+    for q in rest:
         sum_copy(q).start()
         stat_copy(q).start()
-        return carry
-
-    lax.fori_loop(0, n - 1, serve, 0)
 
     def wait_sums(buffer, sem):
         view = buffer.at[pl.ds(2, 2 * n - 2)]
@@ -332,14 +381,12 @@
         for p in range(2):
             origin = listed(2, p * requests + i, 2 * n)
             away = jnp.maximum(origin - 1, 0)
-            k = lax.rem(away, 2)
-            stats = stat_in[lax.div(away, 2)]
-            log = jnp.sum(jnp.where(skew == k * rows, stats, 0.0), axis=1, keepdims=True)
-            factor = jnp.sum(jnp.where(skew == (k + 2) * rows, stats, 0.0), axis=1, keepdims=True)
-            mean = sum_in[away].astype(F32) * factor
-            at = pl.ds(p * rows, rows)
-            means.append(jnp.where(origin > 0, mean, near[i, at]))
-            logs.append(jnp.where(origin > 0, log, near_log[i, at]))
+            moved = origin > 0
+            stats = jnp.where(moved, stat_in[lax.div(away, 2)], near_stat[i])
+            skip = jnp.where(moved, lax.rem(away, 2), p) * rows
+            logs.append(jnp.sum(jnp.where(skew == skip, stats, 0.0), axis=1, keepdims=True))
+            factor = jnp.sum(jnp.where(skew == skip + 2 * rows, stats, 0.0), axis=1, keepdims=True)
+            means.append(jnp.where(moved, sum_in[away].astype(F32), near[i, pl.ds(p * rows, rows)]) * factor)
         at = pl.ds(pl.multiple_of(i * rows, rows), rows)
         means.append(draft[at, :])
         logs.append(draft_log[at, :])
@@ -351,7 +398,7 @@
         squares[i] = jnp.sum((result * result).reshape(steps, heads, HD), axis=1)
         return carry
 
-    lax.fori_loop(0, requests, combine, 0)
+    lax.fori_loop(0, requests, combine, 0, unroll=COMBINE)
 
     tokens = requests * steps
     total_c = jnp.sum(squares[...].reshape(tokens, HD), axis=1, keepdims=True)
@@ -395,16 +442,26 @@
     slots, page, _ = key_pool.shape
     entries = source.shape[0]
     vmem = pl.BlockSpec(memory_space=pltpu.VMEM)
-    smem = pl.BlockSpec(memory_space=pltpu.SMEM)
     anywhere = pl.BlockSpec(memory_space=pl.ANY)
     dma = pltpu.SemaphoreType.DMA
     table = block_table.T
     return pl.pallas_call(
         functools.partial(kernel, n, nz, tp),
         out_shape=jax.ShapeDtypeStruct((requests, steps, width), F32),
-        in_specs=[smem, smem, vmem, vmem, vmem, anywhere, anywhere] + [vmem] * 6,
+        in_specs=[anywhere] * 11,
         out_specs=vmem,
         scratch_shapes=[
+            pltpu.SMEM((2, requests), I32),
+            pltpu.SMEM((1, requests), I32),
+            pltpu.VMEM((requests, steps, width), BF16),
+            pltpu.VMEM((requests, steps, HD), BF16),
+            pltpu.VMEM((requests, steps, HD), BF16),
+            pltpu.VMEM((2, requests), I32),
+            pltpu.VMEM((1, requests), I32),
+            pltpu.VMEM((1, entries), I32),
+            pltpu.VMEM((1, entries), I32),
+            pltpu.VMEM((1, entries), I32),
+            pltpu.VMEM((1, width), F32),
             pltpu.VMEM((slots, page, HD), BF16),
             pltpu.VMEM((slots, page, HD), BF16),
             pltpu.VMEM(((requests + 1) * rows, HD), F32),
@@ -415,7 +472,7 @@
             pltpu.VMEM((n, 1, slots), I32),
             pltpu.VMEM((8, HD), I32),
             pltpu.SMEM((8, HD), I32),
-            pltpu.VMEM((2, n + 8, slots), F32),
+            pltpu.VMEM((n + 8, slots), F32),
             pltpu.VMEM((n, 2 * rows, HD), BF16),
             pltpu.VMEM((n, 2 * rows, HD), BF16),
             pltpu.VMEM((2 * n, rows, HD), jnp.int16),
@@ -423,18 +480,18 @@
             pltpu.VMEM((n, 1, HD), F32),
             pltpu.VMEM((n, 1, HD), F32),
             pltpu.VMEM((requests, 2 * rows, HD), F32),
-            pltpu.VMEM((requests, 2 * rows, HD), F32),
+            pltpu.VMEM((requests, 1, HD), F32),
             pltpu.VMEM((requests * rows, HD), F32),
             pltpu.VMEM((requests * rows, HD), F32),
             pltpu.VMEM(((requests + 1) * rows, HD), F32),
             pltpu.VMEM((requests, steps, HD), F32),
             pltpu.VMEM((requests, steps, HD), F32),
             pltpu.VMEM((tp, 1, HD), F32),
-            dma((2,)), dma, dma, dma, dma, dma((n,)), dma, dma, dma, dma, dma((tp,)), dma((tp,)),
+            dma((13,)), dma, dma, dma, dma, dma((n,)), dma, dma, dma, dma, dma((tp,)), dma((tp,)),
         ],
-        compiler_params=pltpu.CompilerParams(collective_id=0, has_side_effects=True, vmem_limit_bytes=40 * 2**20),
+        compiler_params=pltpu.CompilerParams(collective_id=0, has_side_effects=True, vmem_limit_bytes=56 * 2**20),
     )(
-        table, context, queries, new_keys, new_values, key_pool, value_pool, table,
+        queries, new_keys, new_values, key_pool, value_pool, table,
         context.reshape(1, requests), source.reshape(1, entries), replica.reshape(1, entries), target.reshape(1, entries),
         gain.reshape(1, width),
     )

time: 97.7 us -> 84.1 us (0.86)
  local copies, waits for them, and re-layouts: 10.4 us -> 1.87 us
  Pallas kernels: 86.8 us -> 82.1 us
    unnamed x23 -> x1, local copies, waits for them, and re-layouts: 10.4 us -> 1.87 us
    pallas_call x1, Pallas kernels: 86.8 us -> 82.1 us  [per_device(): pl.pallas_call(functools.partial(kernel, n, nz, tp), out_shape=jax.ShapeD...]
where the time goes in v2:
time: 84.1 us; the launch traced here: 84 us
  Pallas kernels  82.1 us (98%)
  local copies, waits for them, and re-layouts  1.87 us (2%)
    pallas_call x1, Pallas kernels, per_device(): pl.pallas_call(functools.partial(kernel, n, nz, tp), out_shape=jax.ShapeD...  82.1 us
    unnamed x1, local copies, waits for them, and re-layouts  1.87 us

profile of v2, /device:TPU:1, one launch (start us, length us, event | category | flops | bytes accessed | tf_op | source)
XLA Modules:
  0.0 84.0 jit_solution(3670296725185033129)
XLA Ops:
  0.0 82.1 %shard_map.109 = f32[32,4,1024]{2,1,0:T(4,128)} custom-call(bf16[32,4,1024]{2,1,0:T(4,128)(2,1)} %q_hbm.1, bf16[32,4,128]{2,1,0:T(4,128)(2,1)} %nk_hbm.1, bf16[32,4,128]{2,1,0:T(4,128)(2,1)} %nv_hbm.1, bf16[128,64,128]{2,1,0:T(8,128)(2,1)} %kp_ref.1, bf16[128,64,128]{2,1,0:T(8,128)(2,1)} %vp_ref.1, s32[2,32]{1,0:T(2,128)} %bitcast.7, s32[1,32]{1,0:T(1,128)} %bitcast.8, ...), custom_call_target="tpu_custom_call" | custom-call | tf_op jit(solution)/shard_map/pallas_call | solution.py:448
  82.1 1.9 %copy.13 = f32[32,4,1024]{2,1,0:T(4,128)} copy(f32[32,4,1024]{2,1,0:T(4,128)} %shard_map.109) | data formatting | bytes 1048576

commit v3 on v2

--- a/solution.py
+++ b/solution.py
@@ -73,10 +73,10 @@
     out_ref,
     table_s, context_s, q_ref, nk_ref, nv_ref, table_ref, context_ref, source_ref, replica_ref, target_ref, gain_ref,
     kv, vv, qf, qb, nk, nv,
-    note_out, note_in, lists, lists_s, limits,
+    info, lists, lists_s, limits,
     q_out, q_in, sum_out, sum_in, stat_out, stat_in,
     near, near_stat, draft, draft_log, attention, squares, scales, norm_rows,
-    in_sem, list_sem, note_send, note_recv, q_send, q_recv, sum_send, sum_recv, stat_send, stat_recv, norm_send, norm_recv,
+    in_sem, list_sem, row_send, row_recv, column_send, column_recv, q_send, q_recv, sum_send, sum_recv, stat_send, stat_recv, norm_send, norm_recv,
 ):
     ny = n // nz
     requests, steps, width = q_hbm.shape
@@ -95,8 +95,9 @@
     def behind(q):
         return lax.rem(my + ny - lax.div(q, nz), ny) * nz + lax.rem(mz + nz - lax.rem(q, nz), nz)
 
-    def opposite(q):
-        return lax.rem(ny - lax.div(q, nz), ny) * nz + lax.rem(nz - lax.rem(q, nz), nz)
+    def around(base, step, size):
+        total = base + step
+        return jnp.where(total >= size, total - size, total)
 
     def order(step):
         return lax.rem((step + 1) * 27, n)
@@ -111,45 +112,18 @@
         fetch.start()
 
     barrier = pltpu.get_barrier_semaphore()
-
-    def greet(step, carry):
-        pl.semaphore_signal(barrier, inc=1, device_id=(ahead(step + 1), lane_me), device_id_type=MESH)
-        return carry
-
-    lax.fori_loop(0, n - 1, greet, 0)
+    for other in range(1, nz):
+        pl.semaphore_signal(barrier, inc=1, device_id=(my * nz + around(mz, other, nz), lane_me), device_id_type=MESH)
+    for other in range(1, ny):
+        pl.semaphore_signal(barrier, inc=1, device_id=(around(my, other, ny) * nz + mz, lane_me), device_id_type=MESH)
     for other in range(1, tp):
-        pl.semaphore_signal(barrier, inc=1, device_id=(me, lax.rem(lane_me + other, tp)), device_id_type=MESH)
+        pl.semaphore_signal(barrier, inc=1, device_id=(me, around(lane_me, other, tp)), device_id_type=MESH)
 
     for fetch in fetches[0:5]:
         fetch.wait()
 
-    replica = replica_ref[...].astype(F32)
-    source = source_ref[...].astype(F32)
-    target = target_ref[...].astype(F32)
-    square = (entries, entries)
-    replica_c = to_column(replica, entries)
-    same_before = (replica_c == replica) & (iota(square, 0) < iota(square, 1))
-    rank = jnp.sum(jnp.where(same_before, 1.0, 0.0), axis=0, keepdims=True)
-    rank_c = to_column(rank, entries)
-    source_c = to_column(source, entries)
-
-    def vector_peer(q, sign):
-        dy, dz = q // nz, q % nz
-        return (((my + ny + sign * dy) % ny) * nz + (mz + nz + sign * dz) % nz).astype(F32)
-
-    def targets_of(sign):
-        peers = vector_peer(iota((n, entries), 0), sign)
-        found = []
-        for k in range(2):
-            chosen = (peers == replica) & (rank == float(k))
-            found.append(jnp.sum(jnp.where(chosen, target + 1.0, 0.0), axis=1, keepdims=True) - 1.0)
-        return found
-
-    wide = (entries, 2 * n)
-    peers_row = vector_peer(iota(wide, 1) % n, 1)
-    chosen = (replica_c == peers_row) & (rank_c == (iota(wide, 1) // n).astype(F32))
-    source_row = jnp.sum(jnp.where(chosen, source_c, 0.0), axis=0, keepdims=True)
-
+    info[my, mz] = jnp.full((2, HD), -1, I32)
+    info[my, mz, 0:1, 0:entries] = replica_ref[...] * 65536 + target_ref[...]
     context_c = to_column(context_ref[...].astype(F32), requests)
     by_slot = (requests, slots)
     slot_lane = iota(by_slot, 1).astype(F32)
@@ -163,32 +137,50 @@
         valid_row += jnp.sum(jnp.where(here, valid, 0.0), axis=0, keepdims=True)
         place_row += jnp.sum(jnp.where(here, request_c + float(p * requests), 0.0), axis=0, keepdims=True)
 
-    notes = (n, slots)
-    lane = iota(notes, 1).astype(F32)
-    first, second = targets_of(1)
-    marks = jnp.where(lane == first, 65536.0, 0.0) + jnp.where(lane == second, 131072.0, 0.0)
-    code = (valid_row + marks).astype(I32)
-    for q in range(n):
-        note_out[q] = code[q : q + 1, :]
-    first_back, second_back = targets_of(-1)
-    note_in[0] = jnp.zeros((1, slots), I32)
+    info[my, mz, 1:2, 0:slots] = valid_row.astype(I32)
     q_in[0] = jnp.zeros((2 * rows, HD), BF16)
     sum_in[pl.ds(0, 2)] = jnp.zeros((2, rows, HD), jnp.int16)
     stat_in[0] = jnp.zeros((1, 2 * 2 * rows), F32)
 
-    pl.semaphore_wait(barrier, n - 1 + tp - 1)
-
-    def note_copy(q):
+    pl.semaphore_wait(barrier, nz - 1 + ny - 1 + tp - 1)
+
+    def row_copy(other, at):
         return pltpu.make_async_remote_copy(
-            src_ref=note_out.at[q], dst_ref=note_in.at[q], send_sem=note_send, recv_sem=note_recv,
-            device_id=(ahead(q), lane_me), device_id_type=MESH,
-        )
-
-    def send_note(step, carry):
-        note_copy(order(step)).start()
-        return carry
-
-    lax.fori_loop(0, n - 1, send_note, 0)
+            src_ref=info.at[my, at], dst_ref=info.at[my, at], send_sem=row_send.at[other], recv_sem=row_recv.at[other],
+            device_id=(my * nz + around(mz, other, nz), lane_me), device_id_type=MESH,
+        )
+
+    def column_copy(other, at):
+        return pltpu.make_async_remote_copy(
+            src_ref=info.at[at], dst_ref=info.at[at], send_sem=column_send.at[other], recv_sem=column_recv.at[other],
+            device_id=(around(my, other, ny) * nz + mz, lane_me), device_id_type=MESH,
+        )
+
+    for other in range(1, nz):
+        row_copy(other, mz).start()
+
+    replica = replica_ref[...].astype(F32)
+    source = source_ref[...].astype(F32)
+    target = target_ref[...].astype(F32)
+    square = (entries, entries)
+    replica_c = to_column(replica, entries)
+    same_before = (replica_c == replica) & (iota(square, 0) < iota(square, 1))
+    rank = jnp.sum(jnp.where(same_before, 1.0, 0.0), axis=0, keepdims=True)
+    rank_c = to_column(rank, entries)
+    source_c = to_column(source, entries)
+    wide = (entries, 2 * n)
+    chosen = (replica_c == (iota(wide, 1) % n).astype(F32)) & (rank_c == (iota(wide, 1) // n).astype(F32))
+    source_row = jnp.sum(jnp.where(chosen, source_c, 0.0), axis=0, keepdims=True)
+    receiver = iota((n, entries), 0).astype(F32)
+    landings = []
+    for k in range(2):
+        chosen = (receiver == replica) & (rank == float(k))
+        landings.append(jnp.sum(jnp.where(chosen, target + 1.0, 0.0), axis=1, keepdims=True) - 1.0)
+
+    for other in range(1, nz):
+        row_copy(other, around(mz, nz - other, nz)).wait_recv()
+    for other in range(1, ny):
+        column_copy(other, my).start()
 
     fetches[5].wait()
 
@@ -208,15 +200,24 @@
     def wait_all(buffer, sem, count):
         pltpu.make_async_copy(buffer.at[pl.ds(1, count)], buffer.at[pl.ds(1, count)], sem).wait()
 
-    wait_all(note_in, note_recv, n - 1)
-
-    got = note_in[...].reshape(n, slots)
-    mark = got >> 16
-    count = (got & 65535).astype(F32)
-    place_0 = jnp.sum(jnp.where(mark == 1, place_row + 1.0, 0.0), axis=1, keepdims=True) - 1.0
-    place_1 = jnp.sum(jnp.where(mark == 2, place_row + 1.0, 0.0), axis=1, keepdims=True) - 1.0
-    valid_0 = jnp.sum(jnp.where(lane == first_back, count, 0.0), axis=1, keepdims=True)
-    valid_1 = jnp.sum(jnp.where(lane == second_back, count, 0.0), axis=1, keepdims=True)
+    for other in range(1, ny):
+        column_copy(other, around(my, ny - other, ny)).wait_recv()
+
+    words = info[:, :, 0, :].reshape(n, HD)
+    count = info[:, :, 1, 0:slots].reshape(n, slots).astype(F32)
+    place = iota((n, HD), 1)
+    sender = iota((n, HD), 0)
+    here = ((words >> 16) == me) & (sender != me)
+    keyed = (place * 256 + (words & 65535)).astype(F32)
+    first = jnp.min(jnp.where(here, keyed, 1e6), axis=1, keepdims=True)
+    last = jnp.max(jnp.where(here, keyed, -1.0), axis=1, keepdims=True)
+    slot_0 = jnp.where(last >= 0.0, first - 256.0 * jnp.floor(first * (1.0 / 256.0)), -1.0)
+    slot_1 = jnp.where(last > first, last - 256.0 * jnp.floor(last * (1.0 / 256.0)), -1.0)
+    lane = iota((n, slots), 1).astype(F32)
+    place_0 = jnp.sum(jnp.where(lane == slot_0, place_row + 1.0, 0.0), axis=1, keepdims=True) - 1.0
+    place_1 = jnp.sum(jnp.where(lane == slot_1, place_row + 1.0, 0.0), axis=1, keepdims=True) - 1.0
+    valid_0 = jnp.sum(jnp.where(lane == landings[0], count, 0.0), axis=1, keepdims=True)
+    valid_1 = jnp.sum(jnp.where(lane == landings[1], count, 0.0), axis=1, keepdims=True)
     half = lane - jnp.where(lane >= float(2 * rows), float(2 * rows), 0.0)
     limits[0:n] = jnp.where(half < float(rows), valid_0, valid_1)
 
@@ -231,7 +232,8 @@
     )
     by_place = (n, HD)
     place_lane = iota(by_place, 1).astype(F32)
-    distance_2 = 2.0 * iota(by_place, 0).astype(F32)
+    holder = iota(by_place, 0)
+    distance_2 = 2.0 * (((my + ny - holder // nz) % ny) * nz + (mz + nz - holder % nz) % nz).astype(F32)
     origin_row = jnp.sum(
         jnp.where(place_lane == place_0, distance_2 + 1.0, 0.0) + jnp.where(place_lane == place_1, distance_2 + 2.0, 0.0),
         axis=0, keepdims=True,
@@ -255,8 +257,9 @@
 
     def send_queries(step, carry):
         q = order(step)
-        q_out[q, 0:rows] = qb[listed(1, q, requests - 1)]
-        q_out[q, rows : 2 * rows] = qb[listed(1, q + n, requests - 1)]
+        holder = behind(q)
+        q_out[q, 0:rows] = qb[listed(1, holder, requests - 1)]
+        q_out[q, rows : 2 * rows] = qb[listed(1, holder + n, requests - 1)]
         q_copy(q).start()
         return carry
 
@@ -330,8 +333,8 @@
 
     def serve_pair(first_q, second_q):
         pair = (first_q, second_q)
-        pages = [listed(0, q + k * n, slots - 1) for q in pair for k in range(2)]
-        ends = [limits[pl.ds(opposite(q), 1), :] for q in pair]
+        pages = [listed(0, ahead(q) + k * n, slots - 1) for q in pair for k in range(2)]
+        ends = [limits[pl.ds(ahead(q), 1), :] for q in pair]
         maxima, totals, sums = column_sums(
             jnp.concatenate([q_in[q] for q in pair], axis=0),
             [kv[at] for at in pages], [vv[at] for at in pages], jnp.where(own_lane < 2, ends[0], ends[1]),
@@ -430,7 +433,10 @@
 
     for other in range(1, tp):
         norm_copy(other).wait_send()
-    wait_all(note_out, note_send, n - 1)
+    for other in range(1, nz):
+        row_copy(other, mz).wait_send()
+    for other in range(1, ny):
+        column_copy(other, my).wait_send()
     wait_all(q_out, q_send, n - 1)
     wait_sums(sum_out, sum_send)
     wait_all(stat_out, stat_send, n - 1)
@@ -468,8 +474,7 @@
             pltpu.VMEM((requests, rows, HD), BF16),
             pltpu.VMEM((requests * steps, HD), F32),
             pltpu.VMEM((requests * steps, HD), F32),
-            pltpu.VMEM((n, 1, slots), I32),
-            pltpu.VMEM((n, 1, slots), I32),
+            pltpu.VMEM((n // nz, nz, 2, HD), I32),
             pltpu.VMEM((8, HD), I32),
             pltpu.SMEM((8, HD), I32),
             pltpu.VMEM((n + 8, slots), F32),
@@ -487,9 +492,9 @@
             pltpu.VMEM((requests, steps, HD), F32),
             pltpu.VMEM((requests, steps, HD), F32),
             pltpu.VMEM((tp, 1, HD), F32),
-            dma((13,)), dma, dma, dma, dma, dma((n,)), dma, dma, dma, dma, dma((tp,)), dma((tp,)),
+            dma((13,)), dma, dma((nz,)), dma((nz,)), dma((n // nz,)), dma((n // nz,)), dma, dma((n,)), dma, dma, dma, dma, dma((tp,)), dma((tp,)),
         ],
-        compiler_params=pltpu.CompilerParams(collective_id=0, has_side_effects=True, vmem_limit_bytes=56 * 2**20),
+        compiler_params=pltpu.CompilerParams(collective_id=0, has_side_effects=True, vmem_limit_bytes=40 * 2**20),
     )(
         queries, new_keys, new_values, key_pool, value_pool, table,
         context.reshape(1, requests), source.reshape(1, entries), replica.reshape(1, entries), target.reshape(1, entries),

time: 84.1 us -> 93.3 us (1.11)
  local copies, waits for them, and re-layouts: 1.87 us -> 10.4 us
    unnamed x1 -> x23, local copies, waits for them, and re-layouts: 1.87 us -> 10.4 us
where the time goes in v3:
time: 93.3 us; the launch traced here: 92.9 us
  Pallas kernels  82.4 us (88%)
  local copies, waits for them, and re-layouts  10.4 us (11%)
    pallas_call x1, Pallas kernels, per_device(): pl.pallas_call(functools.partial(kernel, n, nz, tp), out_shape=jax.ShapeD...  82.4 us
    unnamed x23, local copies, waits for them, and re-layouts  10.4 us

profile of v3, /device:TPU:1, one launch (start us, length us, event | category | flops | bytes accessed | tf_op | source)
XLA Modules:
  0.0 92.9 jit_solution(11573741245351528119)
XLA Ops:
  0.0 0.0 copy-start
  0.0 1.6 %copy-done = bf16[128,64,128]{2,1,0:T(8,128)(2,1)S(1)} copy-done((bf16[128,64,128]{2,1,0:T(8,128)(2,1)S(1)}, bf16[128,64,128]{2,1,0:T(8,128)(2,1)}, u32[]{:S(2)}) %copy-start) | copy-done | bytes 2097176
  1.6 0.0 copy-start.1
  1.6 1.6 %copy-done.1 = bf16[128,64,128]{2,1,0:T(8,128)(2,1)S(1)} copy-done((bf16[128,64,128]{2,1,0:T(8,128)(2,1)S(1)}, bf16[128,64,128]{2,1,0:T(8,128)(2,1)}, u32[]{:S(2)}) %copy-start.1) | copy-done | bytes 2097176
  3.2 0.0 copy-start.2
  3.2 0.9 %copy-done.2 = bf16[32,4,1024]{2,1,0:T(4,128)(2,1)S(1)} copy-done((bf16[32,4,1024]{2,1,0:T(4,128)(2,1)S(1)}, bf16[32,4,1024]{2,1,0:T(4,128)(2,1)}, u32[]{:S(2)}) %copy-start.2) | copy-done | bytes 262168
  4.1 0.0 copy-start.3
  4.1 0.8 copy-done.3
  4.9 0.0 copy-start.4
  4.9 0.8 copy-done.4
  5.7 0.0 copy-start.5
  5.7 0.7 copy-done.5
  6.3 0.0 copy-start.6
  6.3 0.7 copy-done.6
  7.0 0.0 copy-start.7
  7.0 0.7 copy-done.7
  7.7 0.0 copy-start.8
  7.7 0.7 copy-done.8
  8.3 0.0 copy-start.9
  8.3 0.7 copy-done.9
  9.0 0.0 copy-start.10
  9.0 0.7 copy-done.10
  9.6 82.4 %shard_map.109 = f32[32,4,1024]{2,1,0:T(4,128)S(1)} custom-call(bf16[32,4,1024]{2,1,0:T(4,128)(2,1)S(1)} %copy-done.2, bf16[32,4,128]{2,1,0:T(4,128)(2,1)S(1)} %copy-done.3, bf16[32,4,128]{2,1,0:T(4,128)(2,1)S(1)} %copy-done.4, bf16[128,64,128]{2,1,0:T(8,128)(2,1)S(1)} %copy-done, bf16[128,64,128]{2,1,0:T(8,128)(2,1)S(1)} %copy-done.1, s32[2,32]{1,0:T(2,128)S(1)} %bitcast.7, ...), custom_call_target="tpu_custom_call" | custom-call | tf_op jit(solution)/shard_map/pallas_call | solution.py:454
  92.1 0.8 copy.13
Async XLA Ops:
  0.0 1.6 %copy-start = (bf16[128,64,128]{2,1,0:T(8,128)(2,1)S(1)}, bf16[128,64,128]{2,1,0:T(8,128)(2,1)}, u32[]{:S(2)}) copy-start(bf16[128,64,128]{2,1,0:T(8,128)(2,1)} %kp_ref.1) | copy-start | bytes 6291460
  1.6 1.6 %copy-start.1 = (bf16[128,64,128]{2,1,0:T(8,128)(2,1)S(1)}, bf16[128,64,128]{2,1,0:T(8,128)(2,1)}, u32[]{:S(2)}) copy-start(bf16[128,64,128]{2,1,0:T(8,128)(2,1)} %vp_ref.1) | copy-start | bytes 6291460
  3.2 0.9 %copy-start.2 = (bf16[32,4,1024]{2,1,0:T(4,128)(2,1)S(1)}, bf16[32,4,1024]{2,1,0:T(4,128)(2,1)}, u32[]{:S(2)}) copy-start(bf16[32,4,1024]{2,1,0:T(4,128)(2,1)} %q_hbm.1) | copy-start | bytes 786436
  4.1 0.8 copy-start.3
  4.9 0.8 copy-start.4
  5.7 0.7 copy-start.5
  6.3 0.7 copy-start.6
  7.0 0.7 copy-start.7
  7.7 0.7 copy-start.8
  8.3 0.7 copy-start.9
  9.0 0.7 copy-start.10

commit v4 on v2

--- a/solution.py
+++ b/solution.py
@@ -14,7 +14,9 @@
 TOP = 32767.0
 OWN = 4
 SERVE = 4
+SKIPS = 1
 COMBINE = 4
+STRIDE = 27
 MESH = pl.DeviceIdType.MESH
 I32 = jnp.int32
 F32 = jnp.float32
@@ -67,16 +69,32 @@
     return maxima, totals, sums
 
 
+def reach(n, nz):
+    ny = n // nz
+    near = [q for q in range(1, n) if hops(q, ny, nz) <= (2 if n > 16 else 1)]
+    far, q = [], 0
+    while len(far) < n - 1 - len(near):
+        q = (q + STRIDE) % n
+        if q and q not in near:
+            far.append(q)
+    return near, far
+
+
+def hops(q, ny, nz):
+    y, z = q // nz, q % nz
+    return min(y, ny - y) + min(z, nz - z)
+
+
 def kernel(
     n, nz, tp,
     q_hbm, nk_hbm, nv_hbm, kp_ref, vp_ref, table_hbm, context_hbm, source_hbm, replica_hbm, target_hbm, gain_hbm,
     out_ref,
     table_s, context_s, q_ref, nk_ref, nv_ref, table_ref, context_ref, source_ref, replica_ref, target_ref, gain_ref,
     kv, vv, qf, qb, nk, nv,
-    note_out, note_in, lists, lists_s, limits,
+    near_out, near_in, note_out, note_in, lists, lists_s, sources, sources_s, limits,
     q_out, q_in, sum_out, sum_in, stat_out, stat_in,
     near, near_stat, draft, draft_log, attention, squares, scales, norm_rows,
-    in_sem, list_sem, note_send, note_recv, q_send, q_recv, sum_send, sum_recv, stat_send, stat_recv, norm_send, norm_recv,
+    in_sem, list_sem, near_send, near_recv, note_send, note_recv, q_send, q_recv, sum_send, sum_recv, stat_send, stat_recv, norm_send, norm_recv,
 ):
     ny = n // nz
     requests, steps, width = q_hbm.shape
@@ -99,7 +117,20 @@
         return lax.rem(ny - lax.div(q, nz), ny) * nz + lax.rem(nz - lax.rem(q, nz), nz)
 
     def order(step):
-        return lax.rem((step + 1) * 27, n)
+        return lax.rem((step + 1) * STRIDE, n)
+
+    near_q, far_q = reach(n, nz)
+    far = len(far_q)
+
+    def following(q):
+        for turn in range(SKIPS + 1):
+            there = lax.rem(q + STRIDE, n)
+            if turn > 0:
+                y, z = lax.div(q, nz), lax.rem(q, nz)
+                away = jnp.minimum(y, ny - y) + jnp.minimum(z, nz - z)
+                there = jnp.where(away <= (2 if n > 16 else 1), there, q)
+            q = there
+        return q
 
     moves = [
         (replica_hbm, replica_ref), (source_hbm, source_ref), (target_hbm, target_ref), (table_hbm, table_ref),
@@ -149,6 +180,11 @@
     peers_row = vector_peer(iota(wide, 1) % n, 1)
     chosen = (replica_c == peers_row) & (rank_c == (iota(wide, 1) // n).astype(F32))
     source_row = jnp.sum(jnp.where(chosen, source_c, 0.0), axis=0, keepdims=True)
+
+    sources[...] = jnp.zeros(sources.shape, I32)
+    sources[0:1, 0 : 2 * n] = source_row.astype(I32)
+    source_copy = pltpu.make_async_copy(sources, sources_s, list_sem)
+    source_copy.start()
 
     context_c = to_column(context_ref[...].astype(F32), requests)
     by_slot = (requests, slots)
@@ -172,9 +208,22 @@
         note_out[q] = code[q : q + 1, :]
     first_back, second_back = targets_of(-1)
     note_in[0] = jnp.zeros((1, slots), I32)
-    q_in[0] = jnp.zeros((2 * rows, HD), BF16)
-    sum_in[pl.ds(0, 2)] = jnp.zeros((2, rows, HD), jnp.int16)
-    stat_in[0] = jnp.zeros((1, 2 * 2 * rows), F32)
+    q_at = iota((n, HD), 0)
+    far_number = jnp.zeros((n, HD), F32)
+    near_number = jnp.zeros((n, HD), F32)
+    for at, q in enumerate(far_q):
+        far_number = jnp.where(q_at == q, at + 1.0, far_number)
+    for at, q in enumerate(near_q):
+        near_number = jnp.where(q_at == q, at + 1.0, near_number)
+
+    for fetch in fetches[6:]:
+        fetch.wait()
+    source_copy.wait()
+    for at, q in enumerate(near_q):
+        for k in range(2):
+            page_at = jnp.minimum(jnp.maximum(sources_s[0, q + k * n], 0), slots - 1)
+            near_out[2 * at + k, 0] = kv[page_at]
+            near_out[2 * at + k, 1] = vv[page_at]
 
     pl.semaphore_wait(barrier, n - 1 + tp - 1)
 
@@ -190,6 +239,15 @@
 
     lax.fori_loop(0, n - 1, send_note, 0)
 
+    def near_copy(at):
+        return pltpu.make_async_remote_copy(
+            src_ref=near_out.at[pl.ds(2 * at, 2)], dst_ref=near_in.at[pl.ds(2 * at, 2)], send_sem=near_send.at[at],
+            recv_sem=near_recv.at[at], device_id=(ahead(near_q[at]), lane_me), device_id_type=MESH,
+        )
+
+    for at in range(len(near_q)):
+        near_copy(at).start()
+
     fetches[5].wait()
 
     def spread(i, carry):
@@ -205,10 +263,11 @@
 
     lax.fori_loop(0, requests, narrow, 0)
 
-    def wait_all(buffer, sem, count):
-        pltpu.make_async_copy(buffer.at[pl.ds(1, count)], buffer.at[pl.ds(1, count)], sem).wait()
-
-    wait_all(note_in, note_recv, n - 1)
+    def wait_all(buffer, sem, start, count):
+        view = buffer.at[pl.ds(start, count)]
+        pltpu.make_async_copy(view, view, sem).wait()
+
+    wait_all(note_in, note_recv, 1, n - 1)
 
     got = note_in[...].reshape(n, slots)
     mark = got >> 16
@@ -229,17 +288,16 @@
         jnp.where(lane_2 == distance, request_0, 0.0) + jnp.where(lane_2 == distance + n, request_1, 0.0),
         axis=0, keepdims=True,
     )
-    by_place = (n, HD)
-    place_lane = iota(by_place, 1).astype(F32)
-    distance_2 = 2.0 * iota(by_place, 0).astype(F32)
-    origin_row = jnp.sum(
-        jnp.where(place_lane == place_0, distance_2 + 1.0, 0.0) + jnp.where(place_lane == place_1, distance_2 + 2.0, 0.0),
-        axis=0, keepdims=True,
-    )
+    place_lane = iota((n, HD), 1).astype(F32)
+
+    def origins(number):
+        mine = jnp.where(place_lane == place_0, 1.0, 0.0) + jnp.where(place_lane == place_1, 2.0, 0.0)
+        return jnp.sum(jnp.where((mine > 0.0) & (number > 0.0), 2.0 * number - 2.0 + mine, 0.0), axis=0, keepdims=True)
+
     lists[...] = jnp.zeros(lists.shape, I32)
-    lists[0:1, 0 : 2 * n] = source_row.astype(I32)
+    lists[0:1, 0:HD] = origins(near_number).astype(I32)
     lists[1:2, 0 : 2 * n] = request_row.astype(I32)
-    lists[2:3, :] = origin_row.astype(I32)
+    lists[2:3, :] = origins(far_number).astype(I32)
     list_copy = pltpu.make_async_copy(lists, lists_s, list_sem)
     list_copy.start()
     list_copy.wait()
@@ -247,23 +305,22 @@
     def listed(line, at, limit):
         return jnp.minimum(jnp.maximum(lists_s[line, at], 0), limit)
 
-    def q_copy(q):
+    def q_copy(at, q):
         return pltpu.make_async_remote_copy(
-            src_ref=q_out.at[q], dst_ref=q_in.at[q], send_sem=q_send, recv_sem=q_recv.at[q],
+            src_ref=q_out.at[at], dst_ref=q_in.at[at], send_sem=q_send, recv_sem=q_recv.at[at],
             device_id=(behind(q), lane_me), device_id_type=MESH,
         )
 
-    def send_queries(step, carry):
-        q = order(step)
-        q_out[q, 0:rows] = qb[listed(1, q, requests - 1)]
-        q_out[q, rows : 2 * rows] = qb[listed(1, q + n, requests - 1)]
-        q_copy(q).start()
-        return carry
-
-    lax.fori_loop(0, n - 1, send_queries, 0)
-
-    for fetch in fetches[6:]:
-        fetch.wait()
+    def send_queries(at, q):
+        q_out[at, 0:rows] = qb[listed(1, q, requests - 1)]
+        q_out[at, rows : 2 * rows] = qb[listed(1, q + n, requests - 1)]
+        q_copy(at, q).start()
+        return following(q)
+
+    lax.fori_loop(0, far, send_queries, far_q[0])
+
+    for at in range(len(near_q)):
+        near_copy(at).wait_recv()
     lane_1 = iota((1, HD), 1)
     own_lane = lane_1 // rows
 
@@ -278,11 +335,18 @@
         pair = (2 * step, 2 * step + 1)
         first_context, second_context = context_s[0, pair[0]], context_s[0, pair[1]]
         limit = jnp.where(own_lane < 2, first_context, second_context) - jnp.where(own_lane % 2 == 1, page, 0)
-        pages = [table_s[p, i] for i in pair for p in range(2)]
+        keys, values = [], []
+        for i in pair:
+            for p in range(2):
+                arrived = listed(0, p * requests + i, 2 * len(near_q))
+                landed = jnp.maximum(arrived - 1, 0)
+                at = table_s[p, i]
+                keys.append(jnp.where(arrived > 0, near_in[landed, 0], kv[at]))
+                values.append(jnp.where(arrived > 0, near_in[landed, 1], vv[at]))
         mine = [qb[i] for i in pair]
         maxima, totals, sums = column_sums(
             jnp.concatenate([mine[0], mine[0], mine[1], mine[1]], axis=0),
-            [kv[at] for at in pages], [vv[at] for at in pages], limit.astype(F32),
+            keys, values, limit.astype(F32),
         )
         stats = stat_pair(maxima + jnp.log(totals), 1.0 / totals)
         for at, i in enumerate(pair):
@@ -314,64 +378,58 @@
 
     lax.fori_loop(0, requests // chunk, own_draft, 0, unroll=2)
 
-    def sum_copy(q):
+    def sum_copy(at, q):
         return pltpu.make_async_remote_copy(
-            src_ref=sum_out.at[pl.ds(2 * q, 2)], dst_ref=sum_in.at[pl.ds(2 * q, 2)], send_sem=sum_send, recv_sem=sum_recv,
+            src_ref=sum_out.at[pl.ds(2 * at, 2)], dst_ref=sum_in.at[pl.ds(2 * at, 2)], send_sem=sum_send, recv_sem=sum_recv,
             device_id=(ahead(q), lane_me), device_id_type=MESH,
         )
 
-    def stat_copy(q):
+    def stat_copy(at, q):
         return pltpu.make_async_remote_copy(
-            src_ref=stat_out.at[q], dst_ref=stat_in.at[q], send_sem=stat_send, recv_sem=stat_recv,
+            src_ref=stat_out.at[at], dst_ref=stat_in.at[at], send_sem=stat_send, recv_sem=stat_recv,
             device_id=(ahead(q), lane_me), device_id_type=MESH,
         )
 
     square_1 = iota(blocky, 0) == iota(blocky, 1)
 
-    def serve_pair(first_q, second_q):
-        pair = (first_q, second_q)
-        pages = [listed(0, q + k * n, slots - 1) for q in pair for k in range(2)]
+    def serve_pair(start, pair):
+        pages = [jnp.minimum(jnp.maximum(sources_s[0, q + k * n], 0), slots - 1) for q in pair for k in range(2)]
         ends = [limits[pl.ds(opposite(q), 1), :] for q in pair]
         maxima, totals, sums = column_sums(
-            jnp.concatenate([q_in[q] for q in pair], axis=0),
+            jnp.concatenate([q_in[start], q_in[start + 1]], axis=0),
             [kv[at] for at in pages], [vv[at] for at in pages], jnp.where(own_lane < 2, ends[0], ends[1]),
         )
         largest = jnp.maximum(jnp.max(jnp.abs(sums), axis=1, keepdims=True), 1e-30)
         coded = jnp.round(sums * (TOP / largest)).astype(I32).astype(jnp.int16)
         largest_row = jnp.sum(jnp.where(square_1, largest, 0.0), axis=0, keepdims=True)
         stats = stat_pair(maxima + jnp.log(totals), largest_row / (TOP * totals))
-        for at, q in enumerate(pair):
-            sum_out[pl.ds(2 * q, 2)] = coded[at * 2 * rows : (at + 1) * 2 * rows].reshape(2, rows, HD)
-            stat_out[q] = stats[at]
-
-    def serve(step, carry):
-        qs = [order(step * SERVE + at) for at in range(SERVE)]
-        for q in qs:
-            q_copy(q).wait_recv()
-        for at in range(0, SERVE, 2):
-            serve_pair(qs[at], qs[at + 1])
-        for q in qs:
-            sum_copy(q).start()
-            stat_copy(q).start()
-        return carry
-
-    whole = (n - 2) // SERVE
-    lax.fori_loop(0, whole, serve, 0)
-    rest = [order(step) for step in range(whole * SERVE, n - 1)]
-    for q in rest:
-        q_copy(q).wait_recv()
-    for at in range(0, len(rest), 2):
-        serve_pair(rest[at], rest[at + 1] if at + 1 < len(rest) else 0)
-    for q in rest:
-        sum_copy(q).start()
-        stat_copy(q).start()
-
-    def wait_sums(buffer, sem):
-        view = buffer.at[pl.ds(2, 2 * n - 2)]
-        pltpu.make_async_copy(view, view, sem).wait()
-
-    wait_sums(sum_in, sum_recv)
-    wait_all(stat_in, stat_recv, n - 1)
+        for k in range(2):
+            sum_out[pl.ds(2 * (start + k), 2)] = coded[k * 2 * rows : (k + 1) * 2 * rows].reshape(2, rows, HD)
+            stat_out[start + k] = stats[k]
+
+    def serve_some(start, qs):
+        for at, q in enumerate(qs):
+            q_copy(start + at, q).wait_recv()
+        for at in range(0, len(qs), 2):
+            serve_pair(start + at, (qs[at], qs[at + 1] if at + 1 < len(qs) else 0))
+        for at, q in enumerate(qs):
+            sum_copy(start + at, q).start()
+            stat_copy(start + at, q).start()
+
+    def serve(step, q):
+        qs = [q]
+        for _ in range(SERVE):
+            qs.append(following(qs[-1]))
+        serve_some(step * SERVE, qs[:-1])
+        return qs[-1]
+
+    q_in[far] = jnp.zeros((2 * rows, HD), BF16)
+    whole = (far - 1) // SERVE
+    lax.fori_loop(0, whole, serve, far_q[0])
+    serve_some(whole * SERVE, far_q[whole * SERVE :])
+
+    wait_all(sum_in, sum_recv, 0, 2 * far)
+    wait_all(stat_in, stat_recv, 0, far)
 
     short = (rows, HD)
     skew = iota(short, 1) - iota(short, 0)
@@ -379,7 +437,7 @@
     def combine(i, carry):
         means, logs = [], []
         for p in range(2):
-            origin = listed(2, p * requests + i, 2 * n)
+            origin = listed(2, p * requests + i, 2 * far)
             away = jnp.maximum(origin - 1, 0)
             moved = origin > 0
             stats = jnp.where(moved, stat_in[lax.div(away, 2)], near_stat[i])
@@ -430,10 +488,12 @@
 
     for other in range(1, tp):
         norm_copy(other).wait_send()
-    wait_all(note_out, note_send, n - 1)
-    wait_all(q_out, q_send, n - 1)
-    wait_sums(sum_out, sum_send)
-    wait_all(stat_out, stat_send, n - 1)
+    for at in range(len(near_q)):
+        near_copy(at).wait_send()
+    wait_all(note_out, note_send, 1, n - 1)
+    wait_all(q_out, q_send, 0, far)
+    wait_all(sum_out, sum_send, 0, 2 * far)
+    wait_all(stat_out, stat_send, 0, far)
 
 
 def per_device(n, nz, tp, queries, new_keys, new_values, key_pool, value_pool, block_table, context, source, replica, target, gain):
@@ -445,6 +505,7 @@
     anywhere = pl.BlockSpec(memory_space=pl.ANY)
     dma = pltpu.SemaphoreType.DMA
     table = block_table.T
+    near, far = (len(distances) for distances in reach(n, nz))
     return pl.pallas_call(
         functools.partial(kernel, n, nz, tp),
         out_shape=jax.ShapeDtypeStruct((requests, steps, width), F32),
@@ -468,17 +529,21 @@
             pltpu.VMEM((requests, rows, HD), BF16),
             pltpu.VMEM((requests * steps, HD), F32),
             pltpu.VMEM((requests * steps, HD), F32),
+            pltpu.VMEM((2 * near, 2, page, HD), BF16),
+            pltpu.VMEM((2 * near, 2, page, HD), BF16),
             pltpu.VMEM((n, 1, slots), I32),
             pltpu.VMEM((n, 1, slots), I32),
             pltpu.VMEM((8, HD), I32),
             pltpu.SMEM((8, HD), I32),
+            pltpu.VMEM((8, HD), I32),
+            pltpu.SMEM((8, HD), I32),
             pltpu.VMEM((n + 8, slots), F32),
-            pltpu.VMEM((n, 2 * rows, HD), BF16),
-            pltpu.VMEM((n, 2 * rows, HD), BF16),
-            pltpu.VMEM((2 * n, rows, HD), jnp.int16),
-            pltpu.VMEM((2 * n, rows, HD), jnp.int16),
-            pltpu.VMEM((n, 1, HD), F32),
-            pltpu.VMEM((n, 1, HD), F32),
+            pltpu.VMEM((far + 1, 2 * rows, HD), BF16),
+            pltpu.VMEM((far + 1, 2 * rows, HD), BF16),
+            pltpu.VMEM((2 * far + 2, rows, HD), jnp.int16),
+            pltpu.VMEM((2 * far + 2, rows, HD), jnp.int16),
+            pltpu.VMEM((far + 1, 1, HD), F32),
+            pltpu.VMEM((far + 1, 1, HD), F32),
             pltpu.VMEM((requests, 2 * rows, HD), F32),
             pltpu.VMEM((requests, 1, HD), F32),
             pltpu.VMEM((requests * rows, HD), F32),
@@ -487,7 +552,7 @@
             pltpu.VMEM((requests, steps, HD), F32),
             pltpu.VMEM((requests, steps, HD), F32),
             pltpu.VMEM((tp, 1, HD), F32),
-            dma((13,)), dma, dma, dma, dma, dma((n,)), dma, dma, dma, dma, dma((tp,)), dma((tp,)),
+            dma((13,)), dma, dma((near,)), dma((near,)), dma, dma, dma, dma((far,)), dma, dma, dma, dma, dma((tp,)), dma((tp,)),
         ],
         compiler_params=pltpu.CompilerParams(collective_id=0, has_side_effects=True, vmem_limit_bytes=56 * 2**20),
     )(

time: 84.1 us -> 82.8 us (0.985); the launches traced: 84 us -> 81.1 us
  Pallas kernels: 82.1 us -> 79.2 us
    pallas_call x1, Pallas kernels: 82.1 us -> 79.2 us  [per_device(): pl.pallas_call(functools.partial(kernel, n, nz, tp), out_shape=jax.ShapeD...]
where the time goes in v4:
time: 82.8 us; the launch traced here: 81.1 us
  Pallas kernels  79.2 us (96%)
  local copies, waits for them, and re-layouts  1.87 us (2%)
    pallas_call x1, Pallas kernels, per_device(): pl.pallas_call(functools.partial(kernel, n, nz, tp), out_shape=jax.ShapeD...  79.2 us
    unnamed x1, local copies, waits for them, and re-layouts  1.87 us

profile of v4, /device:TPU:1, one launch (start us, length us, event | category | flops | bytes accessed | tf_op | source)
XLA Modules:
  0.0 81.1 jit_solution(7794779420628693032)
XLA Ops:
  0.0 79.2 %shard_map.109 = f32[32,4,1024]{2,1,0:T(4,128)} custom-call(bf16[32,4,1024]{2,1,0:T(4,128)(2,1)} %q_hbm.1, bf16[32,4,128]{2,1,0:T(4,128)(2,1)} %nk_hbm.1, bf16[32,4,128]{2,1,0:T(4,128)(2,1)} %nv_hbm.1, bf16[128,64,128]{2,1,0:T(8,128)(2,1)} %kp_ref.1, bf16[128,64,128]{2,1,0:T(8,128)(2,1)} %vp_ref.1, s32[2,32]{1,0:T(2,128)} %bitcast.7, s32[1,32]{1,0:T(1,128)} %bitcast.8, ...), custom_call_target="tpu_custom_call" | custom-call | tf_op jit(solution)/shard_map/pallas_call | solution.py:509
  79.2 1.9 %copy.13 = f32[32,4,1024]{2,1,0:T(4,128)} copy(f32[32,4,1024]{2,1,0:T(4,128)} %shard_map.109) | data formatting | bytes 1048576

commit v5 on v4

--- a/solution.py
+++ b/solution.py
@@ -14,7 +14,6 @@
 TOP = 32767.0
 OWN = 4
 SERVE = 4
-SKIPS = 1
 COMBINE = 4
 STRIDE = 27
 MESH = pl.DeviceIdType.MESH
@@ -91,7 +90,7 @@
     out_ref,
     table_s, context_s, q_ref, nk_ref, nv_ref, table_ref, context_ref, source_ref, replica_ref, target_ref, gain_ref,
     kv, vv, qf, qb, nk, nv,
-    near_out, near_in, note_out, note_in, lists, lists_s, sources, sources_s, limits,
+    near_out, near_in, note_out, note_in, lists, lists_s, sources, sources_s, plan_s, limits,
     q_out, q_in, sum_out, sum_in, stat_out, stat_in,
     near, near_stat, draft, draft_log, attention, squares, scales, norm_rows,
     in_sem, list_sem, near_send, near_recv, note_send, note_recv, q_send, q_recv, sum_send, sum_recv, stat_send, stat_recv, norm_send, norm_recv,
@@ -122,15 +121,15 @@
     near_q, far_q = reach(n, nz)
     far = len(far_q)
 
-    def following(q):
-        for turn in range(SKIPS + 1):
-            there = lax.rem(q + STRIDE, n)
-            if turn > 0:
-                y, z = lax.div(q, nz), lax.rem(q, nz)
-                away = jnp.minimum(y, ny - y) + jnp.minimum(z, nz - z)
-                there = jnp.where(away <= (2 if n > 16 else 1), there, q)
-            q = there
-        return q
+    barrier = pltpu.get_barrier_semaphore()
+
+    def greet(step, carry):
+        pl.semaphore_signal(barrier, inc=1, device_id=(ahead(step + 1), lane_me), device_id_type=MESH)
+        return carry
+
+    lax.fori_loop(0, n - 1, greet, 0)
+    for other in range(1, tp):
+        pl.semaphore_signal(barrier, inc=1, device_id=(me, lax.rem(lane_me + other, tp)), device_id_type=MESH)
 
     moves = [
         (replica_hbm, replica_ref), (source_hbm, source_ref), (target_hbm, target_ref), (table_hbm, table_ref),
@@ -141,16 +140,8 @@
     for fetch in fetches:
         fetch.start()
 
-    barrier = pltpu.get_barrier_semaphore()
-
-    def greet(step, carry):
-        pl.semaphore_signal(barrier, inc=1, device_id=(ahead(step + 1), lane_me), device_id_type=MESH)
-        return carry
-
-    lax.fori_loop(0, n - 1, greet, 0)
-    for other in range(1, tp):
-        pl.semaphore_signal(barrier, inc=1, device_id=(me, lax.rem(lane_me + other, tp)), device_id_type=MESH)
-
+    for at, q in enumerate(far_q):
+        plan_s[at] = q
     for fetch in fetches[0:5]:
         fetch.wait()
 
@@ -206,15 +197,26 @@
     code = (valid_row + marks).astype(I32)
     for q in range(n):
         note_out[q] = code[q : q + 1, :]
-    first_back, second_back = targets_of(-1)
     note_in[0] = jnp.zeros((1, slots), I32)
-    q_at = iota((n, HD), 0)
-    far_number = jnp.zeros((n, HD), F32)
-    near_number = jnp.zeros((n, HD), F32)
-    for at, q in enumerate(far_q):
-        far_number = jnp.where(q_at == q, at + 1.0, far_number)
-    for at, q in enumerate(near_q):
-        near_number = jnp.where(q_at == q, at + 1.0, near_number)
+    pl.semaphore_wait(barrier, n - 1 + tp - 1)
+
+    def note_copy(q):
+        return pltpu.make_async_remote_copy(
+            src_ref=note_out.at[q], dst_ref=note_in.at[q], send_sem=note_send, recv_sem=note_recv,
+            device_id=(ahead(q), lane_me), device_id_type=MESH,
+        )
+
+    def send_note(step, carry):
+        note_copy(order(step)).start()
+        return carry
+
+    lax.fori_loop(0, n - 1, send_note, 0)
+
+    def near_copy(at):
+        return pltpu.make_async_remote_copy(
+            src_ref=near_out.at[pl.ds(2 * at, 2)], dst_ref=near_in.at[pl.ds(2 * at, 2)], send_sem=near_send.at[at],
+            recv_sem=near_recv.at[at], device_id=(ahead(near_q[at]), lane_me), device_id_type=MESH,
+        )
 
     for fetch in fetches[6:]:
         fetch.wait()
@@ -225,28 +227,16 @@
             near_out[2 * at + k, 0] = kv[page_at]
             near_out[2 * at + k, 1] = vv[page_at]
 
-    pl.semaphore_wait(barrier, n - 1 + tp - 1)
-
-    def note_copy(q):
-        return pltpu.make_async_remote_copy(
-            src_ref=note_out.at[q], dst_ref=note_in.at[q], send_sem=note_send, recv_sem=note_recv,
-            device_id=(ahead(q), lane_me), device_id_type=MESH,
-        )
-
-    def send_note(step, carry):
-        note_copy(order(step)).start()
-        return carry
-
-    lax.fori_loop(0, n - 1, send_note, 0)
-
-    def near_copy(at):
-        return pltpu.make_async_remote_copy(
-            src_ref=near_out.at[pl.ds(2 * at, 2)], dst_ref=near_in.at[pl.ds(2 * at, 2)], send_sem=near_send.at[at],
-            recv_sem=near_recv.at[at], device_id=(ahead(near_q[at]), lane_me), device_id_type=MESH,
-        )
-
     for at in range(len(near_q)):
         near_copy(at).start()
+    first_back, second_back = targets_of(-1)
+    q_at = iota((n, HD), 0)
+    far_number = jnp.zeros((n, HD), F32)
+    near_number = jnp.zeros((n, HD), F32)
+    for at, q in enumerate(far_q):
+        far_number = jnp.where(q_at == q, at + 1.0, far_number)
+    for at, q in enumerate(near_q):
+        near_number = jnp.where(q_at == q, at + 1.0, near_number)
 
     fetches[5].wait()
 
@@ -274,11 +264,6 @@
     count = (got & 65535).astype(F32)
     place_0 = jnp.sum(jnp.where(mark == 1, place_row + 1.0, 0.0), axis=1, keepdims=True) - 1.0
     place_1 = jnp.sum(jnp.where(mark == 2, place_row + 1.0, 0.0), axis=1, keepdims=True) - 1.0
-    valid_0 = jnp.sum(jnp.where(lane == first_back, count, 0.0), axis=1, keepdims=True)
-    valid_1 = jnp.sum(jnp.where(lane == second_back, count, 0.0), axis=1, keepdims=True)
-    half = lane - jnp.where(lane >= float(2 * rows), float(2 * rows), 0.0)
-    limits[0:n] = jnp.where(half < float(rows), valid_0, valid_1)
-
     line = (n, 2 * n)
     lane_2 = iota(line, 1)
     distance = iota(line, 0)
@@ -288,36 +273,46 @@
         jnp.where(lane_2 == distance, request_0, 0.0) + jnp.where(lane_2 == distance + n, request_1, 0.0),
         axis=0, keepdims=True,
     )
+    lists[...] = jnp.zeros(lists.shape, I32)
+    lists[1:2, 0 : 2 * n] = request_row.astype(I32)
+    list_copy = pltpu.make_async_copy(lists, lists_s, list_sem)
+    list_copy.start()
+    list_copy.wait()
+
+    def listed(line, at, limit):
+        return jnp.minimum(jnp.maximum(lists_s[line, at], 0), limit)
+
+    def q_copy(at, q):
+        return pltpu.make_async_remote_copy(
+            src_ref=q_out.at[at], dst_ref=q_in.at[at], send_sem=q_send, recv_sem=q_recv.at[at],
+            device_id=(behind(q), lane_me), device_id_type=MESH,
+        )
+
+    def send_queries(at, carry):
+        q = plan_s[at]
+        q_out[at, 0:rows] = qb[listed(1, q, requests - 1)]
+        q_out[at, rows : 2 * rows] = qb[listed(1, q + n, requests - 1)]
+        q_copy(at, q).start()
+        return carry
+
+    lax.fori_loop(0, far, send_queries, 0)
+
+    valid_0 = jnp.sum(jnp.where(lane == first_back, count, 0.0), axis=1, keepdims=True)
+    valid_1 = jnp.sum(jnp.where(lane == second_back, count, 0.0), axis=1, keepdims=True)
+    half = lane - jnp.where(lane >= float(2 * rows), float(2 * rows), 0.0)
+    limits[0:n] = jnp.where(half < float(rows), valid_0, valid_1)
+
     place_lane = iota((n, HD), 1).astype(F32)
 
     def origins(number):
         mine = jnp.where(place_lane == place_0, 1.0, 0.0) + jnp.where(place_lane == place_1, 2.0, 0.0)
         return jnp.sum(jnp.where((mine > 0.0) & (number > 0.0), 2.0 * number - 2.0 + mine, 0.0), axis=0, keepdims=True)
 
-    lists[...] = jnp.zeros(lists.shape, I32)
     lists[0:1, 0:HD] = origins(near_number).astype(I32)
-    lists[1:2, 0 : 2 * n] = request_row.astype(I32)
     lists[2:3, :] = origins(far_number).astype(I32)
     list_copy = pltpu.make_async_copy(lists, lists_s, list_sem)
     list_copy.start()
     list_copy.wait()
-
-    def listed(line, at, limit):
-        return jnp.minimum(jnp.maximum(lists_s[line, at], 0), limit)
-
-    def q_copy(at, q):
-        return pltpu.make_async_remote_copy(
-            src_ref=q_out.at[at], dst_ref=q_in.at[at], send_sem=q_send, recv_sem=q_recv.at[at],
-            device_id=(behind(q), lane_me), device_id_type=MESH,
-        )
-
-    def send_queries(at, q):
-        q_out[at, 0:rows] = qb[listed(1, q, requests - 1)]
-        q_out[at, rows : 2 * rows] = qb[listed(1, q + n, requests - 1)]
-        q_copy(at, q).start()
-        return following(q)
-
-    lax.fori_loop(0, far, send_queries, far_q[0])
 
     for at in range(len(near_q)):
         near_copy(at).wait_recv()
@@ -416,16 +411,13 @@
             sum_copy(start + at, q).start()
             stat_copy(start + at, q).start()
 
-    def serve(step, q):
-        qs = [q]
-        for _ in range(SERVE):
-            qs.append(following(qs[-1]))
-        serve_some(step * SERVE, qs[:-1])
-        return qs[-1]
+    def serve(step, carry):
+        serve_some(step * SERVE, [plan_s[step * SERVE + at] for at in range(SERVE)])
+        return carry
 
     q_in[far] = jnp.zeros((2 * rows, HD), BF16)
     whole = (far - 1) // SERVE
-    lax.fori_loop(0, whole, serve, far_q[0])
+    lax.fori_loop(0, whole, serve, 0)
     serve_some(whole * SERVE, far_q[whole * SERVE :])
 
     wait_all(sum_in, sum_recv, 0, 2 * far)
@@ -537,6 +529,7 @@
             pltpu.SMEM((8, HD), I32),
             pltpu.VMEM((8, HD), I32),
             pltpu.SMEM((8, HD), I32),
+            pltpu.SMEM((far + 1,), I32),
             pltpu.VMEM((n + 8, slots), F32),
             pltpu.VMEM((far + 1, 2 * rows, HD), BF16),
             pltpu.VMEM((far + 1, 2 * rows, HD), BF16),

time: 82.8 us -> 81.5 us (0.984); the launches traced: 81.1 us -> 81.4 us
  no operation moved by 1% of the time
where the time goes in v5:
time: 81.5 us; the launch traced here: 81.4 us
  Pallas kernels  79.5 us (98%)
  local copies, waits for them, and re-layouts  1.87 us (2%)
    pallas_call x1, Pallas kernels, per_device(): pl.pallas_call(functools.partial(kernel, n, nz, tp), out_shape=jax.ShapeD...  79.5 us
    unnamed x1, local copies, waits for them, and re-layouts  1.87 us

profile of v5, /device:TPU:1, one launch (start us, length us, event | category | flops | bytes accessed | tf_op | source)
XLA Modules:
  0.0 81.4 jit_solution(2753212378305593844)
XLA Ops:
  0.0 79.5 %shard_map.109 = f32[32,4,1024]{2,1,0:T(4,128)} custom-call(bf16[32,4,1024]{2,1,0:T(4,128)(2,1)} %q_hbm.1, bf16[32,4,128]{2,1,0:T(4,128)(2,1)} %nk_hbm.1, bf16[32,4,128]{2,1,0:T(4,128)(2,1)} %nv_hbm.1, bf16[128,64,128]{2,1,0:T(8,128)(2,1)} %kp_ref.1, bf16[128,64,128]{2,1,0:T(8,128)(2,1)} %vp_ref.1, s32[2,32]{1,0:T(2,128)} %bitcast.7, s32[1,32]{1,0:T(1,128)} %bitcast.8, ...), custom_call_target="tpu_custom_call" | custom-call | tf_op jit(solution)/shard_map/pallas_call | solution.py:501
  79.5 1.9 %copy.13 = f32[32,4,1024]{2,1,0:T(4,128)} copy(f32[32,4,1024]{2,1,0:T(4,128)} %shard_map.109) | data formatting | bytes 1048576

commit v6 on v5

--- a/solution.py
+++ b/solution.py
@@ -14,7 +14,7 @@
 TOP = 32767.0
 OWN = 4
 SERVE = 4
-COMBINE = 4
+COMBINE = 8
 STRIDE = 27
 MESH = pl.DeviceIdType.MESH
 I32 = jnp.int32
@@ -92,7 +92,7 @@
     kv, vv, qf, qb, nk, nv,
     near_out, near_in, note_out, note_in, lists, lists_s, sources, sources_s, plan_s, limits,
     q_out, q_in, sum_out, sum_in, stat_out, stat_in,
-    near, near_stat, draft, draft_log, attention, squares, scales, norm_rows,
+    near, near_stat, draft, draft_log, attention, laid, squares, scales, norm_rows,
     in_sem, list_sem, near_send, near_recv, note_send, note_recv, q_send, q_recv, sum_send, sum_recv, stat_send, stat_recv, norm_send, norm_recv,
 ):
     ny = n // nz
@@ -121,25 +121,27 @@
     near_q, far_q = reach(n, nz)
     far = len(far_q)
 
-    barrier = pltpu.get_barrier_semaphore()
-
-    def greet(step, carry):
-        pl.semaphore_signal(barrier, inc=1, device_id=(ahead(step + 1), lane_me), device_id_type=MESH)
-        return carry
-
-    lax.fori_loop(0, n - 1, greet, 0)
-    for other in range(1, tp):
-        pl.semaphore_signal(barrier, inc=1, device_id=(me, lax.rem(lane_me + other, tp)), device_id_type=MESH)
-
     moves = [
         (replica_hbm, replica_ref), (source_hbm, source_ref), (target_hbm, target_ref), (table_hbm, table_ref),
         (context_hbm, context_ref), (q_hbm, q_ref), (table_hbm, table_s), (context_hbm, context_s), (nk_hbm, nk_ref),
         (nv_hbm, nv_ref), (kp_ref, kv), (vp_ref, vv), (gain_hbm, gain_ref),
     ]
     fetches = [pltpu.make_async_copy(a, b, in_sem.at[at]) for at, (a, b) in enumerate(moves)]
-    for fetch in fetches:
+    for fetch in fetches[0:5]:
         fetch.start()
 
+    barrier = pltpu.get_barrier_semaphore()
+
+    def greet(step, carry):
+        pl.semaphore_signal(barrier, inc=1, device_id=(ahead(step + 1), lane_me), device_id_type=MESH)
+        return carry
+
+    lax.fori_loop(0, n - 1, greet, 0)
+    for other in range(1, tp):
+        pl.semaphore_signal(barrier, inc=1, device_id=(me, lax.rem(lane_me + other, tp)), device_id_type=MESH)
+
+    for fetch in fetches[5:]:
+        fetch.start()
     for at, q in enumerate(far_q):
         plan_s[at] = q
     for fetch in fetches[0:5]:
@@ -387,38 +389,40 @@
 
     square_1 = iota(blocky, 0) == iota(blocky, 1)
 
-    def serve_pair(start, pair):
-        pages = [jnp.minimum(jnp.maximum(sources_s[0, q + k * n], 0), slots - 1) for q in pair for k in range(2)]
-        ends = [limits[pl.ds(opposite(q), 1), :] for q in pair]
+    def serve_pair(pair, qs):
+        pages = [jnp.minimum(jnp.maximum(sources_s[0, q + k * n], 0), slots - 1) for q in qs for k in range(2)]
+        ends = [limits[pl.ds(opposite(q), 1), :] for q in qs]
         maxima, totals, sums = column_sums(
-            jnp.concatenate([q_in[start], q_in[start + 1]], axis=0),
+            jnp.concatenate([q_in[at] for at in pair], axis=0),
             [kv[at] for at in pages], [vv[at] for at in pages], jnp.where(own_lane < 2, ends[0], ends[1]),
         )
         largest = jnp.maximum(jnp.max(jnp.abs(sums), axis=1, keepdims=True), 1e-30)
         coded = jnp.round(sums * (TOP / largest)).astype(I32).astype(jnp.int16)
         largest_row = jnp.sum(jnp.where(square_1, largest, 0.0), axis=0, keepdims=True)
         stats = stat_pair(maxima + jnp.log(totals), largest_row / (TOP * totals))
-        for k in range(2):
-            sum_out[pl.ds(2 * (start + k), 2)] = coded[k * 2 * rows : (k + 1) * 2 * rows].reshape(2, rows, HD)
-            stat_out[start + k] = stats[k]
-
-    def serve_some(start, qs):
-        for at, q in enumerate(qs):
-            q_copy(start + at, q).wait_recv()
-        for at in range(0, len(qs), 2):
-            serve_pair(start + at, (qs[at], qs[at + 1] if at + 1 < len(qs) else 0))
-        for at, q in enumerate(qs):
-            sum_copy(start + at, q).start()
-            stat_copy(start + at, q).start()
+        for k, at in enumerate(pair):
+            sum_out[pl.ds(2 * at, 2)] = coded[k * 2 * rows : (k + 1) * 2 * rows].reshape(2, rows, HD)
+            stat_out[at] = stats[k]
+
+    def serve_some(ats, qs):
+        for at, q in zip(ats, qs):
+            q_copy(at, q).wait_recv()
+        for k in range(0, len(ats), 2):
+            alone = k + 1 == len(ats)
+            serve_pair((ats[k], far if alone else ats[k + 1]), (qs[k], 0 if alone else qs[k + 1]))
+        for at, q in zip(ats, qs):
+            sum_copy(at, q).start()
+            stat_copy(at, q).start()
 
     def serve(step, carry):
-        serve_some(step * SERVE, [plan_s[step * SERVE + at] for at in range(SERVE)])
+        ats = [step * SERVE + turn for turn in range(SERVE)]
+        serve_some(ats, [plan_s[at] for at in ats])
         return carry
 
     q_in[far] = jnp.zeros((2 * rows, HD), BF16)
     whole = (far - 1) // SERVE
     lax.fori_loop(0, whole, serve, 0)
-    serve_some(whole * SERVE, far_q[whole * SERVE :])
+    serve_some(list(range(whole * SERVE, far)), far_q[whole * SERVE :])
 
     wait_all(sum_in, sum_recv, 0, 2 * far)
     wait_all(stat_in, stat_recv, 0, far)
@@ -462,6 +466,14 @@
 
     for other in range(1, tp):
         norm_copy(other).start()
+
+    def lay(i, carry):
+        for h in range(heads):
+            laid[i, :, h * HD : (h + 1) * HD] = attention[pl.ds(i * rows + h, steps, stride=heads), :]
+        return carry
+
+    lax.fori_loop(0, requests, lay, 0)
+
     for other in range(1, tp):
         norm_copy(other).wait_recv()
     total = norm_rows[0]
@@ -473,10 +485,10 @@
     def finish(i, carry):
         for h in range(heads):
             at = slice(h * HD, (h + 1) * HD)
-            out_ref[i, :, at] = attention[pl.ds(i * rows + h, steps, stride=heads), :] * scales[i] * gain_ref[:, at]
-        return carry
-
-    lax.fori_loop(0, requests, finish, 0)
+            out_ref[i, :, at] = laid[i, :, at] * scales[i] * gain_ref[:, at]
+        return carry
+
+    lax.fori_loop(0, requests, finish, 0, unroll=4)
 
     for other in range(1, tp):
         norm_copy(other).wait_send()
@@ -494,13 +506,13 @@
     slots, page, _ = key_pool.shape
     entries = source.shape[0]
     vmem = pl.BlockSpec(memory_space=pltpu.VMEM)
-    anywhere = pl.BlockSpec(memory_space=pl.ANY)
+    anywhere = pl.BlockSpec(memory_space=pltpu.HBM)
     dma = pltpu.SemaphoreType.DMA
     table = block_table.T
     near, far = (len(distances) for distances in reach(n, nz))
     return pl.pallas_call(
         functools.partial(kernel, n, nz, tp),
-        out_shape=jax.ShapeDtypeStruct((requests, steps, width), F32),
+        out_shape=pltpu.VMEM((requests, steps, width), F32),
         in_specs=[anywhere] * 11,
         out_specs=vmem,
         scratch_shapes=[
@@ -542,6 +554,7 @@
             pltpu.VMEM((requests * rows, HD), F32),
             pltpu.VMEM((requests * rows, HD), F32),
             pltpu.VMEM(((requests + 1) * rows, HD), F32),
+            pltpu.VMEM((requests, steps, width), F32),
             pltpu.VMEM((requests, steps, HD), F32),
             pltpu.VMEM((requests, steps, HD), F32),
             pltpu.VMEM((tp, 1, HD), F32),

time: 81.5 us -> 78.9 us (0.968)
  Pallas kernels: 79.5 us -> 78 us
  local copies, waits for them, and re-layouts: 1.87 us -> 0.8 us
    pallas_call x1, Pallas kernels: 79.5 us -> 78 us  [per_device(): pl.pallas_call(functools.partial(kernel, n, nz, tp), out_shape=pltpu.VMEM...]
    unnamed x1, local copies, waits for them, and re-layouts: 1.87 us -> 0.8 us
where the time goes in v6:
time: 78.9 us; the launch traced here: 78.8 us
  Pallas kernels  78 us (99%)
  local copies, waits for them, and re-layouts  0.8 us (1%)
    pallas_call x1, Pallas kernels, per_device(): pl.pallas_call(functools.partial(kernel, n, nz, tp), out_shape=pltpu.VMEM...  78 us

profile of v6, /device:TPU:1, one launch (start us, length us, event | category | flops | bytes accessed | tf_op | source)
XLA Modules:
  0.0 78.8 jit_solution(4072422503111487858)
XLA Ops:
  0.0 78.0 %shard_map.109 = f32[32,4,1024]{2,1,0:T(4,128)S(1)} custom-call(bf16[32,4,1024]{2,1,0:T(4,128)(2,1)} %q_hbm.1, bf16[32,4,128]{2,1,0:T(4,128)(2,1)} %nk_hbm.1, bf16[32,4,128]{2,1,0:T(4,128)(2,1)} %nv_hbm.1, bf16[128,64,128]{2,1,0:T(8,128)(2,1)} %kp_ref.1, bf16[128,64,128]{2,1,0:T(8,128)(2,1)} %vp_ref.1, s32[2,32]{1,0:T(2,128)} %bitcast.7, s32[1,32]{1,0:T(1,128)} %bitcast.8, ...), custom_call_target="tpu_custom_call" | custom-call | tf_op jit(solution)/shard_map/pallas_call | solution.py:513
  78.0 0.8 %copy.13 = f32[32,4,1024]{2,1,0:T(4,128)} copy(f32[32,4,1024]{2,1,0:T(4,128)S(1)} %shard_map.109) | data formatting | bytes 1048576

commit v7 on v6

--- a/solution.py
+++ b/solution.py
@@ -70,7 +70,9 @@
 
 def reach(n, nz):
     ny = n // nz
-    near = [q for q in range(1, n) if hops(q, ny, nz) <= (2 if n > 16 else 1)]
+    most = 2 if n > 16 else 1
+    straight = [q for q in range(1, n) if q % nz == 0 or q // nz == 0]
+    near = [q for q in range(1, n) if hops(q, ny, nz) <= most + (q in straight and n > 16)]
     far, q = [], 0
     while len(far) < n - 1 - len(near):
         q = (q + STRIDE) % n

time: 78.9 us -> 81.9 us (1.038)
  Pallas kernels: 78 us -> 81 us
    pallas_call x1, Pallas kernels: 78 us -> 81 us  [per_device(): pl.pallas_call(functools.partial(kernel, n, nz, tp), out_shape=pltpu.VMEM...]
where the time goes in v7:
time: 81.9 us; the launch traced here: 81.8 us
  Pallas kernels  81 us (99%)
    pallas_call x1, Pallas kernels, per_device(): pl.pallas_call(functools.partial(kernel, n, nz, tp), out_shape=pltpu.VMEM...  81 us

profile of v7, /device:TPU:1, one launch (start us, length us, event | category | flops | bytes accessed | tf_op | source)
XLA Modules:
  0.0 81.8 jit_solution(14082556150509959526)
XLA Ops:
  0.0 81.0 %shard_map.109 = f32[32,4,1024]{2,1,0:T(4,128)S(1)} custom-call(bf16[32,4,1024]{2,1,0:T(4,128)(2,1)} %q_hbm.1, bf16[32,4,128]{2,1,0:T(4,128)(2,1)} %nk_hbm.1, bf16[32,4,128]{2,1,0:T(4,128)(2,1)} %nv_hbm.1, bf16[128,64,128]{2,1,0:T(8,128)(2,1)} %kp_ref.1, bf16[128,64,128]{2,1,0:T(8,128)(2,1)} %vp_ref.1, s32[2,32]{1,0:T(2,128)} %bitcast.7, s32[1,32]{1,0:T(1,128)} %bitcast.8, ...), custom_call_target="tpu_custom_call" | custom-call | tf_op jit(solution)/shard_map/pallas_call | solution.py:515
  81.0 0.8 copy.13
